TPU v7x, 32 devices: a whole 2x2x4 slice. The times are simulated.
32 devices in a mesh: ctx: 8 (over y, x, core), tp: 4 (over z).
Axes of the slice: x: 2, y: 2, z: 4, core: 2. Of those that a mesh axis runs over, the one named last changes fastest.
Arguments:
- residual_in: bfloat16 [4096, 4096], P('ctx', 'tp'), may hold values from -6 to 6
- features: bfloat16 [3, 4096, 2048], P(None, 'ctx', 'tp'), may hold values from -6 to 6
- filter_taps: float32 [2048, 128], P('tp'), may hold values from -1.2 to 1.2
- filter_decay: float32 [2048], P('tp'), may hold values from 0.004 to 0.2
- skip_gain: float32 [2048], P('tp'), may hold values from -3 to 3
- out_weight: bfloat16 [2048, 4096], P('tp'), may hold values from -0.125 to 0.125
- norm_gain: float32 [4096], replicated, may hold values from 0.25 to 1.75
- qkv_weight: bfloat16 [3, 4096, 2048], P(None, None, 'tp'), may hold values from -1 to 1
- doc_lengths: int32 [8], replicated, may hold values from 1 to 3072, 4096 in all
Outputs:
- mixed_stream: bfloat16 [4096, 4096], P('ctx', 'tp')
- attended: bfloat16 [4096, 2048], P('ctx', 'tp')
Inputs may be any that keep to these rules, and one draw needn't show every extreme that they name: doc_lengths sum to 4096; the longest document has exactly 3072 tokens.
All inputs are finite; a program needn't handle non-finite values.
Results may differ from a plain program's by a relative error of at most 0.0085.
Values may be sent and summed in bfloat16 or wider, within the bound.
A program may use at most 128 MiB of HBM per device.

v0:
```python
import jax
import jax.numpy as jnp
from jax import lax
from jax.sharding import PartitionSpec as P

D = 4096
HS = 128


eps = 1e-06


def shifted(value, axis, by):
    devices = lax.axis_size(axis)
    pairs = [(i, i + by) for i in range(devices) if 0 <= i + by < devices]
    return lax.ppermute(value, axis, pairs)


def body(
    residual_in,
    features,
    filter_taps,
    filter_decay,
    skip_gain,
    out_weight,
    norm_gain,
    qkv_weight,
    doc_lengths,
):
    rows = residual_in.shape[0]
    local_width = residual_in.shape[1]
    channels = filter_taps.shape[0]
    span = filter_taps.shape[1]
    query_h = features[0]
    key_h = features[1]
    value_h = features[2]
    edge_keys, edge_values = shifted(
        (key_h[rows - (span - 1) :], value_h[rows - (span - 1) :]), "ctx", 1
    )
    mixed_in = key_h.astype(jnp.float32) * value_h.astype(jnp.float32)
    before = edge_keys.astype(jnp.float32) * edge_values.astype(jnp.float32)
    extended = jnp.concatenate([before, mixed_in], axis=0)
    tap_index = jnp.arange(span, dtype=jnp.float32)
    filt = filter_taps * jnp.exp(-filter_decay[:, None] * tap_index[None, :])
    kernel = filt[:, ::-1].T[:, None, :]
    conv = lax.conv_general_dilated(
        extended[None],
        kernel,
        (1,),
        [(0, 0)],
        dimension_numbers=("NHC", "HIO", "NHC"),
        feature_group_count=channels,
        precision=lax.Precision.HIGHEST,
    )[0]
    gated = (query_h.astype(jnp.float32) * (conv + skip_gain[None, :] * mixed_in)).astype(
        jnp.bfloat16
    )
    offset = lax.axis_index("tp") * local_width
    gain_local = lax.dynamic_slice_in_dim(norm_gain, offset, local_width, 0)
    empty = jnp.zeros((3, rows, qkv_weight.shape[2]), jnp.float32)
    term = jnp.dot(gated, out_weight, preferred_element_type=jnp.float32)
    partial_value = lax.psum_scatter(term, "tp", scatter_dimension=1, tiled=True)
    stream = residual_in.astype(jnp.float32) + partial_value
    squares = lax.psum(jnp.sum(stream * stream, axis=1), "tp")
    scale_rms = lax.rsqrt(squares / D + eps)
    normed = (stream * scale_rms[:, None] * gain_local[None, :]).astype(jnp.bfloat16)
    piece = lax.all_gather(normed, "tp", axis=1, tiled=True)
    weight_rows = lax.slice_in_dim(qkv_weight, 0, piece.shape[1], axis=1)
    projected = empty + jnp.einsum(
        "td,kdh->kth", piece, weight_rows, preferred_element_type=jnp.float32
    )
    mixed_stream = stream.astype(jnp.bfloat16)
    query = projected[0].astype(jnp.bfloat16)
    keys = projected[1].astype(jnp.bfloat16)
    values = projected[2].astype(jnp.bfloat16)
    head_cols = qkv_weight.shape[2]
    heads_local = head_cols // HS
    scale = HS ** (-0.5)
    my_place = lax.axis_index("ctx")
    ends = jnp.cumsum(doc_lengths)
    row_index = jnp.arange(rows, dtype=jnp.int32)
    q_pos = my_place * rows + row_index
    q_seg = jnp.sum((ends[None, :] <= q_pos[:, None]).astype(jnp.int32), axis=1)
    q_heads = query.reshape(rows, heads_local, HS)

    def attend_block(carry, block):
        top, total, accum = carry
        k_block, v_block, k_start = block
        k_pos = k_start + row_index
        k_seg = jnp.sum((ends[None, :] <= k_pos[:, None]).astype(jnp.int32), axis=1)
        allowed = (
            (k_pos[None, :] <= q_pos[:, None])
            & (k_pos[None, :] >= 0)
            & (k_seg[None, :] == q_seg[:, None])
        )
        scores = (
            jnp.einsum(
                "ihd,jhd->hij",
                q_heads,
                k_block.reshape(rows, heads_local, HS),
                preferred_element_type=jnp.float32,
            )
            * scale
        )
        masked = jnp.where(allowed[None], scores, -1e30)
        new_top = jnp.maximum(top, jnp.max(masked, axis=2))
        factor = jnp.exp(top - new_top)
        weights = jnp.where(allowed[None], jnp.exp(scores - new_top[:, :, None]), 0.0)
        total = total * factor + jnp.sum(weights, axis=2)
        summed = jnp.einsum(
            "hij,jhd->hid",
            weights.astype(jnp.bfloat16),
            v_block.reshape(rows, heads_local, HS),
            preferred_element_type=jnp.float32,
        )
        accum = accum * factor[:, :, None] + summed
        return ((new_top, total, accum), None)

    init = (
        jnp.full((heads_local, rows), -1e30, jnp.float32),
        jnp.zeros((heads_local, rows), jnp.float32),
        jnp.zeros((heads_local, rows, HS), jnp.float32),
    )
    carry = init
    k_piece = lax.all_gather(keys, "ctx", axis=0, tiled=True)
    v_piece = lax.all_gather(values, "ctx", axis=0, tiled=True)
    count = k_piece.shape[0] // rows
    k_blocks = k_piece.reshape(count, rows, head_cols)
    v_blocks = v_piece.reshape(count, rows, head_cols)
    starts = jnp.arange(count, dtype=jnp.int32) * rows
    carry, unused = lax.scan(attend_block, carry, (k_blocks, v_blocks, starts))
    top, total, accum = carry
    result = accum / total[:, :, None]
    attended = jnp.transpose(result, (1, 0, 2)).reshape(rows, head_cols).astype(jnp.bfloat16)
    return (mixed_stream, attended)


def solution(mesh):
    return jax.shard_map(
        body,
        mesh=mesh,
        in_specs=(
            P("ctx", "tp"),
            P(None, "ctx", "tp"),
            P("tp", None),
            P("tp"),
            P("tp"),
            P("tp", None),
            P(),
            P(None, None, "tp"),
            P(),
        ),
        out_specs=(P("ctx", "tp"), P("ctx", "tp")),
        check_vma=False,
    )
```

profile of v0, /device:TPU:6, one launch (start us, length us, event | category | flops | bytes accessed | tf_op | source)
XLA Modules:
  0.0 439.1 jit_solution(15499357894898556003)
XLA Ops:
  8.2 1.9 collective-permute-start
  10.2 1.9 collective-permute-start.1
  17.6 14.3 %fusion.39 = f32[1,512,512]{2,0,1:T(1,128)S(1)} fusion(f32[1,639,512]{2,0,1:T(1,128)S(1)} %broadcast_in_dim.28, f32[128,1,512]{2,1,0:T(1,128)S(1)} %copy.30), kind=kOutput, calls=%fused_computation.58 | convolution fusion | flops 402653184 | bytes 2619392 | tf_op jit(solution)/shard_map/conv_general_dilated | solution.py:46
  31.9 6.9 %fusion.32 = f32[512,4096]{1,0:T(8,128)} fusion(bf16[512,4096]{1,0:T(8,128)(2,1)S(1)} %copy-done.1, f32[1,512,512]{2,0,1:T(1,128)S(1)} %fusion.39, f32[512]{0:T(512)S(1)} %copy-done.3, bf16[3,512,512]{2,1,0:T(8,128)(2,1)} %param.12), kind=kOutput, calls=%fused_computation.43 | convolution fusion | flops 2149580800 | bytes 15206400 | tf_op jit(solution)/shard_map/dot_general | solution.py:61
  39.7 145.0 %reduce-scatter.2.cloned.1.call-done = f32[512,1024]{1,0:T(8,128)} async-done(((f32[512,4096]{1,0:T(8,128)}), f32[512,1024]{1,0:T(8,128)}) %reduce-scatter.2.cloned.1.call-update) | async-done | bytes 2097168 | tf_op jit(solution)/shard_map/reduce_scatter | solution.py:62
  184.6 2.1 multiply_reduce_fusion
  186.7 11.4 %psum.7 = f32[512]{0:T(512)S(1)} all-reduce(f32[512]{0:T(512)S(1)} %multiply_reduce_fusion), channel_id=1, replica_groups=mesh['ctx'=8,'tp'=4] {'tp'}, use_global_device_ids=true, to_apply=%region_2.0 | all-reduce | flops 512 | bytes 4096 | tf_op jit(solution)/shard_map/psum | solution.py:64
  198.1 1.7 multiply_convert_fusion
  199.9 79.0 %all-gather.6.cloned.1.call-done = bf16[512,4096]{1,0:T(8,128)(2,1)} async-done(((bf16[512,1024]{1,0:T(8,128)(2,1)}), bf16[512,4096]{1,0:T(8,128)(2,1)}) %all-gather.6.cloned.1.call-update) | async-done | bytes 4194320 | tf_op jit(solution)/shard_map/all_gather | solution.py:67
  278.9 10.9 %fusion.26 = bf16[3,512,512]{1,2,0:T(8,128)(2,1)S(1)} fusion(bf16[3,4096,512]{2,1,0:T(8,128)(2,1)} %param.18, bf16[512,4096]{1,0:T(8,128)(2,1)} %all-gather.6.cloned.1.call-done), kind=kOutput, calls=%fused_computation.35 | convolution fusion | flops 6443237376 | bytes 18350080 | tf_op jit(solution)/shard_map/td,kdh->kth/dot_general | solution.py:69
  292.2 34.0 %all-gather.10.cloned.1.call-done = bf16[1,4096,512]{1,2,0:T(8,128)(2,1)} async-done(((bf16[1,512,512]{1,2,0:T(8,128)(2,1)}), bf16[1,4096,512]{1,2,0:T(8,128)(2,1)}) %all-gather.10.cloned.1.call-update) | async-done | bytes 4194320 | tf_op jit(solution)/shard_map/all_gather | solution.py:126
  326.2 4.4 %copy.43 = bf16[64,8,8,512]{3,2,1,0:T(8,128)(2,1)S(1)} copy(bf16[64,8,8,512]{3,1,2,0:T(8,128)(2,1)} %bitcast.101) | data formatting | bytes 8388608
  330.6 3.4 copy.34
  334.0 31.4 %all-gather.8.cloned.1.call-done = bf16[1,4096,512]{1,2,0:T(8,128)(2,1)} async-done(((bf16[1,512,512]{1,2,0:T(8,128)(2,1)}), bf16[1,4096,512]{1,2,0:T(8,128)(2,1)}) %all-gather.8.cloned.1.call-update) | async-done | bytes 4194320 | tf_op jit(solution)/shard_map/all_gather | solution.py:125
  365.4 4.4 %copy.42 = bf16[64,8,8,512]{3,2,1,0:T(8,128)(2,1)S(1)} copy(bf16[64,8,8,512]{3,1,2,0:T(8,128)(2,1)} %bitcast.102) | data formatting | bytes 8388608
  369.8 3.4 copy.32
  373.2 58.2 %while.15 = (s32[]{:T(128)}, f32[4,512]{1,0:T(4,128)S(1)}, f32[4,512]{1,0:T(4,128)S(1)}, f32[4,512,128]{2,1,0:T(8,128)S(1)}, s32[8]{0:T(128)S(1)}, /*index=5*/s3...) while((s32[]{:T(128)}, f32[4,512]{1,0:T(4,128)S(1)}, ...), condition=%wide.region_9.10_spmd.clone, body=%wide.region_5.9_spmd.clone.sunk | while | flops 550264320 | bytes 19547340 | solution.py:131
  378.8 1.7 fusion.63
  386.1 1.7 fusion.63
  393.4 1.7 fusion.63
  400.7 1.7 fusion.63
  407.9 1.7 fusion.63
  415.2 1.7 fusion.63
  422.5 1.7 fusion.63
  (130 shorter events, 56.7 us)
Async XLA Ops:
  7.2 177.5 %reduce-scatter.2.cloned.1.call-start = ((), (), s32[]{:S(2)}) async-start(), calls=%async_computation.1 | async-start | bytes 10485760 | tf_op jit(solution)/shard_map/reduce_scatter | solution.py:62
  8.2 7.5 %collective-permute-start = (bf16[127,512]{1,0:T(8,128)(2,1)S(1)}, bf16[127,512]{1,0:T(8,128)(2,1)S(1)}, u32[]{:S(2)}, u32[]{:S(2)}) collective-permute-start(bf16[127,512]{1,0:T(8,128)(2,1)S(1)} %get-tuple-element.176), channel_id=1, source_target_pairs={{0,4},{4,8},{8,12},{12,16},{16,20},{20,24},{24,28},{1,5},{5,9},{9,... | collective-permute-start | bytes 390152 | tf_op jit(solution)/shard_map/ppermute | solution.py:16
  10.2 6.3 %collective-permute-start.1 = (bf16[127,512]{1,0:T(8,128)(2,1)S(1)}, bf16[127,512]{1,0:T(8,128)(2,1)S(1)}, u32[]{:S(2)}, u32[]{:S(2)}) collective-permute-start(bf16[127,512]{1,0:T(8,128)(2,1)S(1)} %get-tuple-element.177), channel_id=1, source_target_pairs={{0,4},{4,8},{8,12},{12,16},{16,20},{20,24},{24,28},{1,5},{5,9},{9,... | collective-permute-start | bytes 390152 | tf_op jit(solution)/shard_map/ppermute | solution.py:16
  17.6 14.3 %copy-start.1 = (bf16[512,4096]{1,0:T(8,128)(2,1)S(1)}, bf16[512,4096]{1,0:T(8,128)(2,1)}, u32[]{:S(2)}) copy-start(bf16[512,4096]{1,0:T(8,128)(2,1)} %param.16) | copy-start | bytes 12582916
  17.6 14.3 %copy-start.3 = (f32[512]{0:T(512)S(1)}, f32[512]{0:T(512)}, u32[]{:S(2)}) copy-start(f32[512]{0:T(512)} %param.15) | copy-start | bytes 6148
  38.8 145.8 %copy-start.2 = (bf16[512,1024]{1,0:T(8,128)(2,1)S(1)}, bf16[512,1024]{1,0:T(8,128)(2,1)}, u32[]{:S(2)}) copy-start(bf16[512,1024]{1,0:T(8,128)(2,1)} %param.11) | copy-start | bytes 3145732
  38.8 240.1 %all-gather.6.cloned.1.call-start = ((), (), s32[]{:S(2)}) async-start(), calls=%async_computation.2 | async-start | bytes 5242880 | tf_op jit(solution)/shard_map/all_gather | solution.py:67
  184.6 13.5 %copy-start = (f32[512,1024]{1,0:T(8,128)S(1)}, f32[512,1024]{1,0:T(8,128)}, u32[]{:S(2)}) copy-start(f32[512,1024]{1,0:T(8,128)} %reduce-scatter.2.cloned.1.call-done) | copy-start | bytes 6291460
  199.8 126.4 %all-gather.10.cloned.1.call-start = ((), (), s32[]{:S(2)}) async-start(), calls=%async_computation.4 | async-start | bytes 4718592 | tf_op jit(solution)/shard_map/all_gather | solution.py:126
  289.9 1.8 copy-start.4
  291.0 74.4 %all-gather.8.cloned.1.call-start = ((), (), s32[]{:S(2)}) async-start(), calls=%async_computation.3 | async-start | bytes 4718592 | tf_op jit(solution)/shard_map/all_gather | solution.py:125
Sparse Core Ops, SparseCore 0:
  39.0 145.6 reduce-scatter.1
  200.0 78.8 all-gather.5
  291.1 35.0 all-gather.9
  327.9 37.4 all-gather.7
where the time goes:
time: 442 us; the launch traced here: 439 us
  waiting for transfers between devices  290 us (66%)
  matrix products  53.5 us (12%)
  local copies, waits for them, and re-layouts  35.2 us (8%)
  other arithmetic  29.8 us (7%)
  between operations  14 us (3%)
  blocking collectives  11.4 us (3%)
    reduce_scatter x1, waiting for transfers between devices, body(): lax.psum_scatter(term, 'tp', scatter_dimension=1, tiled=True)  145 us
    all_gather x1, waiting for transfers between devices, body(): piece = lax.all_gather(normed, 'tp', axis=1, tiled=True)  79 us
    all_gather x1, waiting for transfers between devices, body(): v_piece = lax.all_gather(values, 'ctx', axis=0, tiled=True)  34 us
    all_gather x1, waiting for transfers between devices, body(): k_piece = lax.all_gather(keys, 'ctx', axis=0, tiled=True)  31.4 us
    unnamed x15, local copies, waits for them, and re-layouts  15.9 us
    dynamic_slice x16, local copies, waits for them, and re-layouts, body(): carry, unused = lax.scan(attend_block, carry, (k_blocks, v_blocks, starts))  14.9 us
    conv_general_dilated x1, matrix products, body(): lax.conv_general_dilated(extended[None], kernel, (1,), [(0, 0)], dimensio...  14.3 us
    dot_general x8, matrix products, attend_block(): jnp.einsum('hij,jhd->hid', weights.astype(jnp.bfloat16), v_block.reshape(...  13.3 us
  transfers between devices with their start and end apart: 6, of which 5 were waited for; matrix products, arithmetic and copies ran while one was open for 3% of the time, Pallas kernels for 0%

commit v1 on v0

v1 whole, which is shorter than its diff:
```python
import functools
import jax
import jax.numpy as jnp
from jax import lax
from jax.experimental import pallas as pl
from jax.experimental.pallas import tpu as pltpu
from jax.sharding import PartitionSpec as P

D = 4096
HS = 128
LOG2E = 1.4426950408889634


eps = 1e-06


def flip(place, by):
    out = place
    bit = 1
    while bit <= by:
        if by & bit:
            out = out + bit - 2 * bit * ((place // bit) % 2)
        bit *= 2
    return out


def plane_kernel(devices, k_ref, v_ref, k_out, v_out, own_sem, send_sem, recv_sem, mate_send, mate_recv):
    me = lax.axis_index("ctx")
    chips = devices // 2
    rows = k_ref.shape[0]
    chip = me // 2
    core = me % 2
    mate = chip * 2 + 1 - core
    partners = [flip(chip, d) * 2 + core for d in range(1, chips)]

    barrier = pltpu.get_barrier_semaphore()
    for other in partners + [mate]:
        pl.semaphore_signal(barrier, inc=1, device_id={"ctx": other}, device_id_type=pl.DeviceIdType.MESH)
    pl.semaphore_wait(barrier, chips)

    outs = (k_out, v_out)
    ins = (k_ref, v_ref)

    def slot(b, place):
        return outs[b].at[pl.ds(pl.multiple_of(place * rows, rows), rows), :]

    def to_partner(b, d, src, place, target):
        return pltpu.make_async_remote_copy(
            src_ref=src, dst_ref=slot(b, place), send_sem=send_sem.at[b, d], recv_sem=recv_sem.at[b, d],
            device_id={"ctx": target}, device_id_type=pl.DeviceIdType.MESH)

    def to_mate(b, d, src, place):
        return pltpu.make_async_remote_copy(
            src_ref=src, dst_ref=slot(b, place), send_sem=mate_send.at[b, d], recv_sem=mate_recv.at[b, d],
            device_id={"ctx": mate}, device_id_type=pl.DeviceIdType.MESH)

    relayed = chips == 4
    direct = (1, 2) if relayed else tuple(range(1, chips))
    for b in range(2):
        for d in direct:
            to_partner(b, d, ins[b], me, partners[d - 1]).start()
        to_mate(b, 0, ins[b], me).start()
        pltpu.make_async_copy(ins[b], slot(b, me), own_sem.at[b]).start()
    for b in range(2):
        for d in direct:
            place = partners[d - 1]
            to_partner(b, d, slot(b, place), place, place).wait_recv()
            to_mate(b, d, slot(b, place), place).start()
            if relayed:

                @pl.when(core == d - 1)
                def _():
                    to_partner(b, 3, slot(b, place), place, partners[2 - d]).start()
    for b in range(2):
        if relayed:
            place = partners[2]
            to_partner(b, 3, slot(b, place), place, place).wait_recv()
            to_mate(b, 3, slot(b, place), place).start()
    for b in range(2):
        for d in range(1, chips):
            to_partner(b, d, ins[b], me, partners[d - 1]).wait_send()
        for d in range(chips):
            place = flip(chip, d) * 2 + 1 - core
            to_mate(b, d, slot(b, place), place).wait()
        pltpu.make_async_copy(ins[b], slot(b, me), own_sem.at[b]).wait()


def gather_plane(keys, values, devices):
    rows, cols = keys.shape
    chips = devices // 2
    full = jax.ShapeDtypeStruct((devices * rows, cols), keys.dtype)
    return pl.pallas_call(
        functools.partial(plane_kernel, devices),
        out_shape=(full, full),
        in_specs=[pl.BlockSpec(memory_space=pl.ANY)] * 2,
        out_specs=[pl.BlockSpec(memory_space=pl.ANY)] * 2,
        scratch_shapes=[
            pltpu.SemaphoreType.DMA((2,)),
            pltpu.SemaphoreType.DMA((2, chips)),
            pltpu.SemaphoreType.DMA((2, chips)),
            pltpu.SemaphoreType.DMA((2, chips)),
            pltpu.SemaphoreType.DMA((2, chips)),
        ],
        compiler_params=pltpu.CompilerParams(collective_id=1, has_side_effects=True),
        name="gather_keys_values",
    )(keys, values)


def attention_kernel(block, bounds, q_ref, k_ref, v_ref, low_ref, out_ref):
    rows = q_ref.shape[0]
    first = bounds[0]
    low = low_ref[...]
    q = q_ref[...]
    row = lax.broadcasted_iota(jnp.int32, (rows, block), 0) + first
    column = lax.broadcasted_iota(jnp.int32, (rows, block), 1)

    def step(at, carry):
        top, total, accum = carry
        start = pl.multiple_of(at * block, block)
        k = k_ref[pl.ds(start, block), :]
        v = v_ref[pl.ds(start, block), :]
        scores = lax.dot_general(q, k, (((1,), (1,)), ((), ())), preferred_element_type=jnp.float32)
        scores = scores * (HS ** (-0.5) * LOG2E)
        place = column + start
        allowed = (place <= row) & (place >= low)
        masked = jnp.where(allowed, scores, -1e30)
        new_top = jnp.maximum(top, jnp.max(masked, axis=1, keepdims=True))
        factor = jnp.exp2(top - new_top)
        weights = jnp.where(allowed, jnp.exp2(masked - new_top), 0.0)
        total = total * factor + jnp.sum(weights, axis=1, keepdims=True)
        accum = accum * factor + jnp.dot(weights.astype(jnp.bfloat16), v, preferred_element_type=jnp.float32)
        return new_top, total, accum

    init = (
        jnp.full((rows, 1), -1e30, jnp.float32),
        jnp.zeros((rows, 1), jnp.float32),
        jnp.zeros((rows, HS), jnp.float32),
    )
    top, total, accum = lax.fori_loop(bounds[1] // block, (first + rows) // block, step, init)
    out_ref[...] = (accum / total).astype(out_ref.dtype)


def attention(query, k_all, v_all, low, first):
    rows, cols = query.shape
    tokens = k_all.shape[0]
    heads = cols // HS
    bounds = jnp.stack([first, low[0]]).astype(jnp.int32)
    return pl.pallas_call(
        functools.partial(attention_kernel, rows),
        out_shape=jax.ShapeDtypeStruct((rows, cols), jnp.bfloat16),
        grid_spec=pltpu.PrefetchScalarGridSpec(
            num_scalar_prefetch=1,
            grid=(heads,),
            in_specs=[
                pl.BlockSpec((rows, HS), lambda h, b: (0, h)),
                pl.BlockSpec((tokens, HS), lambda h, b: (0, h)),
                pl.BlockSpec((tokens, HS), lambda h, b: (0, h)),
                pl.BlockSpec((rows, 1), lambda h, b: (0, 0)),
            ],
            out_specs=pl.BlockSpec((rows, HS), lambda h, b: (0, h)),
        ),
        compiler_params=pltpu.CompilerParams(vmem_limit_bytes=48 * 1024 * 1024),
        name="attention",
    )(bounds, query, k_all, v_all, low[:, None])


def shifted(value, axis, by):
    devices = lax.axis_size(axis)
    pairs = [(i, i + by) for i in range(devices) if 0 <= i + by < devices]
    return lax.ppermute(value, axis, pairs)


def body(
    residual_in,
    features,
    filter_taps,
    filter_decay,
    skip_gain,
    out_weight,
    norm_gain,
    qkv_weight,
    doc_lengths,
):
    rows = residual_in.shape[0]
    local_width = residual_in.shape[1]
    channels = filter_taps.shape[0]
    span = filter_taps.shape[1]
    query_h = features[0]
    key_h = features[1]
    value_h = features[2]
    edge_keys, edge_values = shifted(
        (key_h[rows - (span - 1) :], value_h[rows - (span - 1) :]), "ctx", 1
    )
    mixed_in = key_h.astype(jnp.float32) * value_h.astype(jnp.float32)
    before = edge_keys.astype(jnp.float32) * edge_values.astype(jnp.float32)
    extended = jnp.concatenate([before, mixed_in], axis=0)
    tap_index = jnp.arange(span, dtype=jnp.float32)
    filt = filter_taps * jnp.exp(-filter_decay[:, None] * tap_index[None, :])
    kernel = filt[:, ::-1].T[:, None, :]
    conv = lax.conv_general_dilated(
        extended[None],
        kernel,
        (1,),
        [(0, 0)],
        dimension_numbers=("NHC", "HIO", "NHC"),
        feature_group_count=channels,
        precision=lax.Precision.HIGHEST,
    )[0]
    gated = (query_h.astype(jnp.float32) * (conv + skip_gain[None, :] * mixed_in)).astype(
        jnp.bfloat16
    )
    offset = lax.axis_index("tp") * local_width
    gain_local = lax.dynamic_slice_in_dim(norm_gain, offset, local_width, 0)
    parts = lax.axis_size("ctx")
    planes = lax.axis_size("tp")
    share = channels // parts
    mine = lax.dynamic_slice_in_dim(out_weight, lax.axis_index("ctx") * share, share, 0)
    moved = lax.all_to_all(mine, "tp", split_axis=1, concat_axis=0, tiled=True)
    columns = lax.all_gather(moved, "ctx", axis=0, tiled=False)
    columns = columns.reshape(parts, planes, share, local_width).transpose(1, 0, 2, 3)
    columns = columns.reshape(planes * channels, local_width)
    gated_all = lax.all_gather(gated, "tp", axis=1, tiled=True)
    stream = residual_in.astype(jnp.float32) + jnp.dot(gated_all, columns, preferred_element_type=jnp.float32)
    mixed_stream = stream.astype(jnp.bfloat16)
    scaled = (stream * gain_local[None, :]).astype(jnp.bfloat16)
    squares = lax.psum(jnp.sum(stream * stream, axis=1), "tp")
    scale_rms = lax.rsqrt(squares / D + eps)
    piece = lax.all_gather(scaled, "tp", axis=1, tiled=True)

    def project(weight):
        product = jnp.dot(piece, weight, preferred_element_type=jnp.float32)
        return (product * scale_rms[:, None]).astype(jnp.bfloat16)

    query = project(qkv_weight[0])
    keys = project(qkv_weight[1])
    values = project(qkv_weight[2])
    ends = jnp.cumsum(doc_lengths)
    first = lax.axis_index("ctx") * rows
    q_pos = first + jnp.arange(rows, dtype=jnp.int32)
    low = jnp.max(jnp.where(ends[None, :] <= q_pos[:, None], ends[None, :], 0), axis=1).astype(jnp.int32)
    k_all, v_all = gather_plane(keys, values, parts)
    attended = attention(query, k_all, v_all, low, first)
    return (mixed_stream, attended)


def solution(mesh):
    return jax.shard_map(
        body,
        mesh=mesh,
        in_specs=(
            P("ctx", "tp"),
            P(None, "ctx", "tp"),
            P("tp", None),
            P("tp"),
            P("tp"),
            P("tp", None),
            P(),
            P(None, None, "tp"),
            P(),
        ),
        out_specs=(P("ctx", "tp"), P("ctx", "tp")),
        check_vma=False,
    )
```

time: 442 us -> 292 us (0.66)
  waiting for transfers between devices: 290 us -> 124 us
  Pallas kernels: 0 us -> 69 us
  other arithmetic: 29.8 us -> 3.55 us
  local copies, waits for them, and re-layouts: 35.2 us -> 9.42 us
  blocking collectives: 11.4 us -> 28.9 us
  matrix products: 53.5 us -> 39 us
    reduce_scatter x1 -> x0, waiting for transfers between devices: 145 us -> none  [body(): lax.psum_scatter(term, 'tp', scatter_dimension=1, tiled=True)]
    pallas_call x0 -> x2, Pallas kernels: none -> 69 us  [the longest x1 38.7 us: gather_plane(): pl.pallas_call(functools.partial(plane_kernel, devices), out_shape=(full,...]
    all_gather x3, waiting for transfers between devices: 144 us -> 119 us  [the longest x1 68.3 us: body(): piece = lax.all_gather(scaled, 'tp', axis=1, tiled=True)]
    all_to_all x0 -> x1, blocking collectives: none -> 19.3 us  [body(): moved = lax.all_to_all(mine, 'tp', split_axis=1, concat_axis=0, tiled=True)]
    unnamed x15 -> x16, local copies, waits for them, and re-layouts: 15.9 us -> 0.04 us
    dot_general x18 -> x4, matrix products: 39.3 us -> 24.7 us  [the longest x3 18 us: project(): product = jnp.dot(piece, weight, preferred_element_type=jnp.float32)]
    dynamic_slice x16 -> x1, local copies, waits for them, and re-layouts: 14.9 us -> 1.2 us  [body(): lax.dynamic_slice_in_dim(out_weight, lax.axis_index('ctx') * share, share...]
    reduce_sum x18 -> x0, other arithmetic: 10.1 us -> none  [the longest x8 7.23 us: attend_block(): total = total * factor + jnp.sum(weights, axis=2)]
  transfers between devices with their start and end apart: 6 -> 5, of which waited for: 5 -> 5; matrix products, arithmetic and copies ran while one was open for 3% -> 9% of each run, Pallas kernels for 0% -> 0%
where the time goes in v1:
time: 292 us
  waiting for transfers between devices  124 us (42%)
  Pallas kernels  69 us (24%)
  matrix products  39 us (13%)
  blocking collectives  28.9 us (10%)
  between operations  14 us (5%)
  local copies, waits for them, and re-layouts  9.42 us (3%)
  starting transfers between devices  3.96 us (1%)
  other arithmetic  3.55 us (1%)
    all_gather x1, waiting for transfers between devices, body(): piece = lax.all_gather(scaled, 'tp', axis=1, tiled=True)  68.3 us
    all_gather x1, waiting for transfers between devices, body(): gated_all = lax.all_gather(gated, 'tp', axis=1, tiled=True)  44.1 us
    pallas_call x1, Pallas kernels, gather_plane(): pl.pallas_call(functools.partial(plane_kernel, devices), out_shape=(full,...  38.7 us
    pallas_call x1, Pallas kernels, attention(): pl.pallas_call(functools.partial(attention_kernel, rows), out_shape=jax.S...  30.4 us
    all_to_all x1, blocking collectives, body(): moved = lax.all_to_all(mine, 'tp', split_axis=1, concat_axis=0, tiled=True)  19.3 us
    dot_general x3, matrix products, project(): product = jnp.dot(piece, weight, preferred_element_type=jnp.float32)  18 us
    conv_general_dilated x1, matrix products, body(): lax.conv_general_dilated(extended[None], kernel, (1,), [(0, 0)], dimensio...  14.3 us
    psum x1, blocking collectives, body(): squares = lax.psum(jnp.sum(stream * stream, axis=1), 'tp')  9.58 us
  transfers between devices with their start and end apart: 5, of which 5 were waited for; matrix products, arithmetic and copies ran while one was open for 9% of the time, Pallas kernels for 0%

profile of v1, /device:TPU:6, one launch (start us, length us, event | category | flops | bytes accessed | tf_op | source)
XLA Modules:
  0.0 291.8 jit_solution(8267555865017740467)
XLA Ops:
  7.2 1.2 constant_dynamic-slice_fusion
  8.5 19.3 %all_to_all.16 = bf16[64,4,1024]{2,0,1:T(8,128)(2,1)} all-to-all(bf16[64,4,1024]{2,0,1:T(8,128)(2,1)S(1)} %bitcast.67), channel_id=1, replica_groups=mesh['ctx'=8,'tp'=4] {'tp'}, dimensions={1} | all-to-all | bytes 1048576 | tf_op jit(solution)/shard_map/all_to_all | solution.py:218
  27.8 1.0 slice_bitcast_fusion.1
  28.9 1.9 collective-permute-start.1
  30.8 1.9 collective-permute-start
  33.6 1.6 collective-permute-done.1
  35.2 3.6 %collective-permute-done = bf16[127,512]{1,0:T(8,128)(2,1)} collective-permute-done((bf16[127,512]{1,0:T(8,128)(2,1)S(1)}, bf16[127,512]{1,0:T(8,128)(2,1)}, u32[]{:S(2)}, u32[]{:S(2)}) %collective-permute-start) | collective-permute-done | bytes 130080 | tf_op jit(solution)/shard_map/ppermute | solution.py:170
  38.8 0.9 convert_multiply_fusion
  39.9 0.9 broadcast_in_dim.12
  40.8 14.3 %fusion.29 = f32[1,512,512]{2,0,1:T(1,128)S(1)} fusion(f32[1,639,512]{2,0,1:T(1,128)S(1)} %broadcast_in_dim.12, f32[128,1,512]{2,1,0:T(1,128)S(1)} %copy.26), kind=kOutput, calls=%fused_computation.33 | convolution fusion | flops 402653184 | bytes 2619392 | tf_op jit(solution)/shard_map/conv_general_dilated | solution.py:200
  55.1 1.1 fusion.28
  56.3 6.5 %all-gather.6.cloned.1.call-done = bf16[8,256,1024]{2,1,0:T(8,128)(2,1)} async-done(((bf16[1,256,1024]{2,1,0:T(8,128)(2,1)}), bf16[8,256,1024]{2,1,0:T(8,128)(2,1)}) %all-gather.6.cloned.1.call-update) | async-done | bytes 4194320 | tf_op jit(solution)/shard_map/all_gather | solution.py:219
  62.8 5.0 %copy.28 = bf16[4,8,64,1024]{3,2,1,0:T(8,128)(2,1)} copy(bf16[4,8,64,1024]{3,2,0,1:T(8,128)(2,1)} %bitcast.63) | data formatting | bytes 8388608 | tf_op jit(solution)/shard_map/transpose | solution.py:220
  67.7 44.1 %all-gather.4.cloned.1.call-done = bf16[512,2048]{1,0:T(8,128)(2,1)} async-done(((bf16[512,512]{1,0:T(8,128)(2,1)}), bf16[512,2048]{1,0:T(8,128)(2,1)}) %all-gather.4.cloned.1.call-update) | async-done | bytes 2097168 | tf_op jit(solution)/shard_map/all_gather | solution.py:222
  111.8 6.7 %multiply_reduce_fusion = (f32[512]{0:T(512)S(1)}, bf16[512,1024]{1,0:T(8,128)(2,1)}, bf16[512,1024]{1,0:T(8,128)(2,1)}) fusion(f32[1024]{0:T(1024)S(1)} %dynamic-slice-done, bf16[512,2048]{1,0:T(8,128)(2,1)} %all-gather.4.cloned.1.call-done, bf16[2048,1024]{1,0:T(8,128)(2,1)} %bitcast.64, bf16[512,1024]{1,0:T(8,128)(2,1)S(1)} %copy-done.6), kind=kOutput, calls=%fused_computation.9 | convolution fusion | flops 2151153152 | bytes 9443328 | tf_op jit(solution)/shard_map/dot_general | solution.py:223
  118.8 0.6 slice.42
  119.5 0.8 pad_add_fusion.bounds
  120.3 9.6 %psum.7 = f32[512]{0:T(512)S(1)} all-reduce(f32[512]{0:T(512)S(1)} %get-tuple-element.6), channel_id=1, replica_groups=mesh['ctx'=8,'tp'=4] {'tp'}, use_global_device_ids=true, to_apply=%region_3.4 | all-reduce | flops 512 | bytes 4096 | tf_op jit(solution)/shard_map/psum | solution.py:226
  129.9 68.3 %all-gather.8.cloned.1.call-done = bf16[512,4096]{1,0:T(8,128)(2,1)} async-done(((bf16[512,1024]{1,0:T(8,128)(2,1)}), bf16[512,4096]{1,0:T(8,128)(2,1)}) %all-gather.8.cloned.1.call-update) | async-done | bytes 4194320 | tf_op jit(solution)/shard_map/all_gather | solution.py:228
  198.2 6.7 %fusion.21.k_ref = bf16[512,512]{1,0:T(8,128)(2,1)} fusion(bf16[512,4096]{1,0:T(8,128)(2,1)} %all-gather.8.cloned.1.call-done, bf16[3,4096,512]{2,1,0:T(8,128)(2,1)} %param.16, f32[512]{0:T(512)S(1)} %add_rsqrt_fusion), kind=kOutput, calls=%fused_computation.17 | convolution fusion | flops 2148007936 | bytes 8914944 | tf_op jit(solution)/shard_map/dot_general | solution.py:231
  204.9 5.4 %fusion.18.v_ref = bf16[512,512]{1,0:T(8,128)(2,1)} fusion(bf16[512,4096]{1,0:T(8,128)(2,1)S(1)} %copy-done.5, bf16[3,4096,512]{2,1,0:T(8,128)(2,1)} %param.16, f32[512]{0:T(512)S(1)} %add_rsqrt_fusion), kind=kOutput, calls=%fused_computation.16 | convolution fusion | flops 2148007936 | bytes 8914944 | tf_op jit(solution)/shard_map/dot_general | solution.py:231
  210.3 38.7 %gather_keys_values.1 = (bf16[4096,512]{1,0:T(8,128)(2,1)}, bf16[4096,512]{1,0:T(8,128)(2,1)}) custom-call(bf16[512,512]{1,0:T(8,128)(2,1)} %fusion.21.k_ref, bf16[512,512]{1,0:T(8,128)(2,1)} %fusion.18.v_ref), custom_call_target="tpu_custom_call" | custom-call | tf_op jit(solution)/shard_map/gather_keys_values/pallas_call | solution.py:92
  249.0 5.9 %fusion.24.q_ref = bf16[512,512]{1,0:T(8,128)(2,1)S(1)} fusion(bf16[512,4096]{1,0:T(8,128)(2,1)} %all-gather.8.cloned.1.call-done, bf16[3,4096,512]{2,1,0:T(8,128)(2,1)} %param.16, f32[512]{0:T(512)S(1)} %add_rsqrt_fusion), kind=kOutput, calls=%fused_computation.18 | convolution fusion | flops 2148007936 | bytes 8914944 | tf_op jit(solution)/shard_map/dot_general | solution.py:231
  254.9 30.4 %attention.1 = bf16[512,512]{1,0:T(8,128)(2,1)} custom-call(s32[2]{0:T(128)S(1)} %pad_add_fusion.bounds, bf16[512,512]{1,0:T(8,128)(2,1)S(1)} %fusion.24.q_ref, bf16[4096,512]{1,0:T(8,128)(2,1)S(1)} %copy-done, bf16[4096,512]{1,0:T(8,128)(2,1)} %get-tuple-element.5.v_ref, s32[512,1]{1,0:T(8,128)S(1)} %copy.29.low_ref), custom_call_target="tpu_custom_call" | custom-call | tf_op jit(solution)/shard_map/attention/pallas_call | solution.py:148
  (36 shorter events, 1.6 us)
Async XLA Ops:
  7.2 25.6 %copy-start.1 = (bf16[3,512,512]{2,1,0:T(8,128)(2,1)S(1)}, bf16[3,512,512]{2,1,0:T(8,128)(2,1)}, u32[]{:S(2)}) copy-start(bf16[3,512,512]{2,1,0:T(8,128)(2,1)} %param.10) | copy-start | bytes 4718596
  7.2 25.6 %copy-start.3 = (f32[512]{0:T(512)S(1)}, f32[512]{0:T(512)}, u32[]{:S(2)}) copy-start(f32[512]{0:T(512)} %param.12) | copy-start | bytes 6148
  7.2 25.7 %copy-start.2 = (f32[512,128]{1,0:T(8,128)S(1)}, f32[512,128]{1,0:T(8,128)}, u32[]{:S(2)}) copy-start(f32[512,128]{1,0:T(8,128)} %param.11) | copy-start | bytes 786436
  7.2 55.6 %all-gather.6.cloned.1.call-start = ((), (), s32[]{:S(2)}) async-start(), calls=%async_computation.2 | async-start | bytes 4718592 | tf_op jit(solution)/shard_map/all_gather | solution.py:219
  27.8 84.0 %all-gather.4.cloned.1.call-start = ((), (), s32[]{:S(2)}) async-start(), calls=%async_computation.1 | async-start | bytes 2621440 | tf_op jit(solution)/shard_map/all_gather | solution.py:222
  28.9 6.3 %collective-permute-start.1 = (bf16[127,512]{1,0:T(8,128)(2,1)S(1)}, bf16[127,512]{1,0:T(8,128)(2,1)S(1)}, u32[]{:S(2)}, u32[]{:S(2)}) collective-permute-start(bf16[127,512]{1,0:T(8,128)(2,1)S(1)} %get-tuple-element.10), channel_id=1, source_target_pairs={{0,4},{4,8},{8,12},{12,16},{16,20},{20,24},{24,28},{1,5},{5,9},{9,... | collective-permute-start | bytes 390152 | tf_op jit(solution)/shard_map/ppermute | solution.py:170
  30.8 8.0 %collective-permute-start = (bf16[127,512]{1,0:T(8,128)(2,1)S(1)}, bf16[127,512]{1,0:T(8,128)(2,1)}, u32[]{:S(2)}, u32[]{:S(2)}) collective-permute-start(bf16[127,512]{1,0:T(8,128)(2,1)S(1)} %get-tuple-element.9), channel_id=1, source_target_pairs={{0,4},{4,8},{8,12},{12,16},{16,20},{20,24},{24,28},{1,5},{5,9},{9,... | collective-permute-start | bytes 390152 | tf_op jit(solution)/shard_map/ppermute | solution.py:170
  40.8 14.3 %copy-start.4 = (f32[512]{0:T(512)S(1)}, f32[512]{0:T(512)}, u32[]{:S(2)}) copy-start(f32[512]{0:T(512)} %param.13) | copy-start | bytes 6148
  56.2 141.9 %all-gather.8.cloned.1.call-start = ((), (), s32[]{:S(2)}) async-start(), calls=%async_computation.3 | async-start | bytes 5242880 | tf_op jit(solution)/shard_map/all_gather | solution.py:228
  62.8 49.0 %dynamic-slice-start = ((f32[4096]{0:T(1024)}, s32[]{:T(128)}), f32[1024]{0:T(1024)S(1)}, s32[]{:S(2)}) async-start(f32[4096]{0:T(1024)} %param.15, s32[]{:T(128)} %select_n.12), calls=%async_computation.4 | async-start | bytes 8704 | tf_op jit(solution)/shard_map/dynamic_slice | solution.py:213
  62.8 49.0 %copy-start.6 = (bf16[512,1024]{1,0:T(8,128)(2,1)S(1)}, bf16[512,1024]{1,0:T(8,128)(2,1)}, u32[]{:S(2)}) copy-start(bf16[512,1024]{1,0:T(8,128)(2,1)} %param.9) | copy-start | bytes 3145732
  111.8 6.7 %copy-start.7 = (s32[8]{0:T(128)S(1)}, s32[8]{0:T(128)}, u32[]{:S(2)}) copy-start(s32[8]{0:T(128)} %param.17) | copy-start | bytes 100
  198.2 6.7 %copy-start.5 = (bf16[512,4096]{1,0:T(8,128)(2,1)S(1)}, bf16[512,4096]{1,0:T(8,128)(2,1)}, u32[]{:S(2)}) copy-start(bf16[512,4096]{1,0:T(8,128)(2,1)} %all-gather.8.cloned.1.call-done) | copy-start | bytes 12582916
  249.0 5.9 %copy-start = (bf16[4096,512]{1,0:T(8,128)(2,1)S(1)}, bf16[4096,512]{1,0:T(8,128)(2,1)}, u32[]{:S(2)}) copy-start(bf16[4096,512]{1,0:T(8,128)(2,1)} %get-tuple-element.4.k_ref) | copy-start | bytes 12582916
Sparse Core Ops, SparseCore 0:
  27.9 34.8 all-gather.5
  64.9 46.8 all-gather.3
  118.6 79.4 all-gather.7

commit v2 on v1

v2 whole, which is shorter than its diff:
```python
import functools
import jax
import jax.numpy as jnp
from jax import lax
from jax.experimental import pallas as pl
from jax.experimental.pallas import tpu as pltpu
from jax.sharding import PartitionSpec as P

D = 4096
HS = 128
LOG2E = 1.4426950408889634


eps = 1e-06


def flip(place, by):
    out = place
    bit = 1
    while bit <= by:
        if by & bit:
            out = out + bit - 2 * bit * ((place // bit) % 2)
        bit *= 2
    return out


def send(src, dst, sent, landed, device):
    return pltpu.make_async_remote_copy(
        src_ref=src, dst_ref=dst, send_sem=sent, recv_sem=landed,
        device_id=device, device_id_type=pl.DeviceIdType.MESH)


def greet(others):
    barrier = pltpu.get_barrier_semaphore()
    for other in others:
        pl.semaphore_signal(barrier, inc=1, device_id=other, device_id_type=pl.DeviceIdType.MESH)
    pl.semaphore_wait(barrier, len(others))


def deal_kernel(devices, planes, g_ref, w_ref, g_out, w_out, own_sem, g_send, g_recv, z_send, z_recv, p_send, p_recv, m_send, m_recv):
    me = lax.axis_index("ctx")
    z = lax.axis_index("tp")
    chips = devices // 2
    tokens, wide = g_ref.shape
    depth = w_ref.shape[0]
    width = w_out.shape[1]
    rows, half = depth // chips, width // 2
    chip = me // 2
    core = me % 2
    mate = chip * 2 + 1 - core
    partners = [flip(chip, d) * 2 + core for d in range(1, chips)]
    others = [(z + s) % planes for s in range(1, planes)]
    greet([{"ctx": p} for p in partners] + [{"ctx": mate}] + [{"tp": t} for t in others])

    def slot(origin, from_chip, from_core):
        return w_out.at[
            pl.ds(pl.multiple_of(origin * depth + from_chip * rows, rows), rows),
            pl.ds(pl.multiple_of(from_core * half, half), half)]

    def g_slot(origin):
        return g_out.at[:, pl.ds(pl.multiple_of(origin * wide, wide), wide)]

    def to_plane(target):
        src = w_ref.at[
            pl.ds(pl.multiple_of(chip * rows, rows), rows),
            pl.ds(pl.multiple_of(target * width + core * half, half), half)]
        return send(src, slot(z, chip, core), z_send.at[target], z_recv.at[z], {"tp": target})

    def from_plane(origin):
        place = slot(origin, chip, core)
        return send(place, place, z_send.at[origin], z_recv.at[origin], {"tp": origin})

    def to_partner(s, d, from_chip, target):
        place = slot(others[s], from_chip, core)
        return send(place, place, p_send.at[s, d], p_recv.at[s, d], {"ctx": target})

    def to_mate(s, d, from_core):
        place = slot(others[s], flip(chip, d), from_core)
        return send(place, place, m_send.at[s, d], m_recv.at[s, d], {"ctx": mate})

    def hop(origin, sent, target):
        place = g_slot(origin)
        return send(place, place, g_send.at[sent], g_recv.at[origin], {"tp": target})

    def first_hop(sent, target):
        return send(g_ref, g_slot(z), g_send.at[sent], g_recv.at[z], {"tp": target})

    for s in range(planes - 1):
        to_plane(others[s]).start()

    @pl.when(z + 1 < planes)
    def _():
        first_hop(planes, z + 1).start()

    @pl.when(z > 0)
    def _():
        first_hop(planes + 1, z - 1).start()

    own = pltpu.make_async_copy(g_ref, g_slot(z), own_sem.at[0])
    own.start()
    kept = pltpu.make_async_copy(
        w_ref.at[:, pl.ds(pl.multiple_of(z * width, width), width)],
        w_out.at[pl.ds(pl.multiple_of(z * depth, depth), depth), :], own_sem.at[1])
    kept.start()

    def relay(s):
        @pl.when(z - s >= 0)
        def _():
            hop(z - s, z - s, z).wait_recv()

            @pl.when(z + 1 < planes)
            def _():
                hop(z - s, z - s, z + 1).start()

        @pl.when(z + s < planes)
        def _():
            hop(z + s, z + s, z).wait_recv()

            @pl.when(z > 0)
            def _():
                hop(z + s, z + s, z - 1).start()

    relayed = chips == 4
    direct = (1, 2) if relayed else tuple(range(1, chips))
    for s in range(planes - 1):
        from_plane(others[s]).wait_recv()
        for d in direct:
            to_partner(s, d, chip, partners[d - 1]).start()
        to_mate(s, 0, core).start()
    relay(1)
    for s in range(planes - 1):
        for d in direct:
            to_partner(s, d, flip(chip, d), partners[d - 1]).wait_recv()
            to_mate(s, d, core).start()
            if relayed:

                @pl.when(core == d - 1)
                def _():
                    to_partner(s, 3, flip(chip, d), partners[2 - d]).start()
    for s in range(2, planes):
        relay(s)
    for s in range(planes - 1):
        if relayed:
            to_partner(s, 3, flip(chip, 3), partners[2]).wait_recv()
            to_mate(s, 3, core).start()
    for s in range(planes - 1):
        to_plane(others[s]).wait_send()
        for d in range(1, chips):
            to_partner(s, d, flip(chip, d), partners[d - 1]).wait_send()
        for d in range(chips):
            to_mate(s, d, core).wait_send()
            to_mate(s, d, 1 - core).wait_recv()

    @pl.when(z + 1 < planes)
    def _():
        first_hop(planes, z + 1).wait_send()

    @pl.when(z > 0)
    def _():
        first_hop(planes + 1, z - 1).wait_send()

    for s in range(1, planes):

        @pl.when((z - s >= 0) & (z + 1 < planes))
        def _():
            hop(z - s, z - s, z + 1).wait_send()

        @pl.when((z + s < planes) & (z > 0))
        def _():
            hop(z + s, z + s, z - 1).wait_send()

    own.wait()
    kept.wait()


def deal(gated, out_weight, devices, planes):
    tokens, wide = gated.shape
    depth, full = out_weight.shape
    chips = devices // 2
    dma = pltpu.SemaphoreType.DMA
    return pl.pallas_call(
        functools.partial(deal_kernel, devices, planes),
        out_shape=(
            jax.ShapeDtypeStruct((tokens, planes * wide), gated.dtype),
            jax.ShapeDtypeStruct((planes * depth, full // planes), out_weight.dtype),
        ),
        in_specs=[pl.BlockSpec(memory_space=pl.ANY)] * 2,
        out_specs=[pl.BlockSpec(memory_space=pl.ANY)] * 2,
        scratch_shapes=[
            dma((2,)), dma((planes + 2,)), dma((planes,)), dma((planes,)), dma((planes,)),
            dma((planes - 1, chips)), dma((planes - 1, chips)), dma((planes - 1, chips)), dma((planes - 1, chips)),
        ],
        compiler_params=pltpu.CompilerParams(collective_id=2, has_side_effects=True),
        name="deal_gated_and_columns",
    )(gated, out_weight)


def attention_kernel(devices, q_ref, k_ref, v_ref, low_ref, out_ref, k_all, v_all, top_ref, total_ref, accum_ref,
                     own_sem, send_sem, recv_sem, mate_send, mate_recv):
    me = lax.axis_index("ctx")
    chips = devices // 2
    rows, cols = q_ref.shape
    chip = me // 2
    core = me % 2
    mate = chip * 2 + 1 - core
    partners = [flip(chip, d) * 2 + core for d in range(1, chips)]
    greet([{"ctx": p} for p in partners] + [{"ctx": mate}])
    outs = (k_all, v_all)
    ins = (k_ref, v_ref)

    def slot(b, place):
        return outs[b].at[pl.ds(pl.multiple_of(place * rows, rows), rows), :]

    def to_partner(b, d, src, place, target):
        return send(src, slot(b, place), send_sem.at[b, d], recv_sem.at[b, d], {"ctx": target})

    def to_mate(b, d, src, place):
        return send(src, slot(b, place), mate_send.at[b, d], mate_recv.at[b, d], {"ctx": mate})

    pair = min(2 * HS, cols)
    pairs = cols // pair

    def attend(place, at):
        start = pl.multiple_of(place * rows, rows)
        row = lax.broadcasted_iota(jnp.int32, (rows, rows), 0) + me * rows
        column = lax.broadcasted_iota(jnp.int32, (rows, rows), 1) + start
        allowed = (column <= row) & (column >= low_ref[...])
        for inner in range(pair // HS):
            lanes = pl.ds(pl.multiple_of(at * pair + inner * HS, HS), HS)
            head = at * (pair // HS) + inner
            scores = lax.dot_general(
                q_ref[:, lanes], k_all[pl.ds(start, rows), lanes], (((1,), (1,)), ((), ())),
                preferred_element_type=jnp.float32)
            masked = jnp.where(allowed, scores * (HS ** (-0.5) * LOG2E), -1e30)
            top = top_ref[head]
            new_top = jnp.maximum(top, jnp.max(masked, axis=1, keepdims=True))
            factor = jnp.exp2(top - new_top)
            weights = jnp.exp2(masked - new_top)
            total_ref[head] = total_ref[head] * factor + jnp.sum(weights, axis=1, keepdims=True)
            accum_ref[:, lanes] = accum_ref[:, lanes] * factor + jnp.dot(
                weights.astype(jnp.bfloat16), v_all[pl.ds(start, rows), lanes], preferred_element_type=jnp.float32)
            top_ref[head] = new_top

    def attend_chip(from_chip, first_core):
        def step(i, unused):
            place = from_chip * 2 + (first_core + i // pairs) % 2

            @pl.when(place <= me)
            def _():
                attend(place, i % pairs)

            return unused

        lax.fori_loop(0, 2 * pairs, step, 0)

    for b in range(2):
        for d in ((1, 2) if chips == 4 else tuple(range(1, chips))):
            to_partner(b, d, ins[b], me, partners[d - 1]).start()
        to_mate(b, 0, ins[b], me).start()
        pltpu.make_async_copy(ins[b], slot(b, me), own_sem.at[b]).start()
    top_ref[...] = jnp.full(top_ref.shape, -1e20, jnp.float32)
    total_ref[...] = jnp.zeros(total_ref.shape, jnp.float32)
    accum_ref[...] = jnp.zeros(accum_ref.shape, jnp.float32)

    def mate_landed(d):
        for b in range(2):
            place = flip(chip, d) * 2 + 1 - core
            to_mate(b, d, slot(b, place), place).wait_recv()

    def partner_landed(d):
        for b in range(2):
            place = partners[d - 1]
            to_partner(b, d, slot(b, place), place, place).wait_recv()
            to_mate(b, d, slot(b, place), place).start()
            if chips == 4 and d < 3:

                @pl.when(core == d - 1)
                def _():
                    to_partner(b, 3, slot(b, place), place, partners[2 - d]).start()

    for b in range(2):
        pltpu.make_async_copy(ins[b], slot(b, me), own_sem.at[b]).wait()
    mate_landed(0)
    attend_chip(chip, core)
    if chips == 4:
        for d in (1, 2):
            partner_landed(d)
        for d in (1, 2):
            mate_landed(d)

        def both(d, unused):
            from_chip = (1 - d) * flip(chip, 1) + d * flip(chip, 2)
            attend_chip(from_chip, 0)
            return unused

        lax.fori_loop(0, 2, both, 0)
        partner_landed(3)
        mate_landed(3)
        attend_chip(flip(chip, 3), 0)
    else:
        for d in range(1, chips):
            partner_landed(d)
        for d in range(1, chips):
            mate_landed(d)

        def later(d, unused):
            attend_chip((chip + d) % chips, 0)
            return unused

        lax.fori_loop(1, chips, later, 0)
    for head in range(cols // HS):
        lanes = pl.ds(head * HS, HS)
        out_ref[:, lanes] = (accum_ref[:, lanes] / total_ref[head]).astype(out_ref.dtype)
    for b in range(2):
        for d in range(1, chips):
            to_partner(b, d, ins[b], me, partners[d - 1]).wait_send()
        for d in range(chips):
            to_mate(b, d, ins[b], me).wait_send()


def attention(query, keys, values, low, devices):
    rows, cols = query.shape
    chips = devices // 2
    dma = pltpu.SemaphoreType.DMA
    return pl.pallas_call(
        functools.partial(attention_kernel, devices),
        out_shape=jax.ShapeDtypeStruct((rows, cols), jnp.bfloat16),
        in_specs=[pl.BlockSpec(memory_space=pltpu.VMEM)] * 4,
        out_specs=pl.BlockSpec(memory_space=pltpu.VMEM),
        scratch_shapes=[
            pltpu.VMEM((devices * rows, cols), jnp.bfloat16),
            pltpu.VMEM((devices * rows, cols), jnp.bfloat16),
            pltpu.VMEM((cols // HS, rows, 1), jnp.float32),
            pltpu.VMEM((cols // HS, rows, 1), jnp.float32),
            pltpu.VMEM((rows, cols), jnp.float32),
            dma((2,)), dma((2, chips)), dma((2, chips)), dma((2, chips)), dma((2, chips)),
        ],
        compiler_params=pltpu.CompilerParams(
            collective_id=1, has_side_effects=True, vmem_limit_bytes=48 * 1024 * 1024),
        name="attention",
    )(query, keys, values, low[:, None])


def shifted(value, axis, by):
    devices = lax.axis_size(axis)
    pairs = [(i, i + by) for i in range(devices) if 0 <= i + by < devices]
    return lax.ppermute(value, axis, pairs)


def body(
    residual_in,
    features,
    filter_taps,
    filter_decay,
    skip_gain,
    out_weight,
    norm_gain,
    qkv_weight,
    doc_lengths,
):
    rows = residual_in.shape[0]
    local_width = residual_in.shape[1]
    channels = filter_taps.shape[0]
    span = filter_taps.shape[1]
    query_h = features[0]
    key_h = features[1]
    value_h = features[2]
    edge_keys, edge_values = shifted(
        (key_h[rows - (span - 1) :], value_h[rows - (span - 1) :]), "ctx", 1
    )
    mixed_in = key_h.astype(jnp.float32) * value_h.astype(jnp.float32)
    before = edge_keys.astype(jnp.float32) * edge_values.astype(jnp.float32)
    extended = jnp.concatenate([before, mixed_in], axis=0)
    tap_index = jnp.arange(span, dtype=jnp.float32)
    filt = filter_taps * jnp.exp(-filter_decay[:, None] * tap_index[None, :])
    kernel = filt[:, ::-1].T[:, None, :]
    conv = lax.conv_general_dilated(
        extended[None],
        kernel,
        (1,),
        [(0, 0)],
        dimension_numbers=("NHC", "HIO", "NHC"),
        feature_group_count=channels,
        precision=lax.Precision.HIGHEST,
    )[0]
    gated = (query_h.astype(jnp.float32) * (conv + skip_gain[None, :] * mixed_in)).astype(
        jnp.bfloat16
    )
    offset = lax.axis_index("tp") * local_width
    gain_local = lax.dynamic_slice_in_dim(norm_gain, offset, local_width, 0)
    parts = lax.axis_size("ctx")
    gated_all, columns = deal(gated, out_weight, parts, lax.axis_size("tp"))
    stream = residual_in.astype(jnp.float32) + jnp.dot(gated_all, columns, preferred_element_type=jnp.float32)
    mixed_stream = stream.astype(jnp.bfloat16)
    scaled = (stream * gain_local[None, :]).astype(jnp.bfloat16)
    squares = lax.psum(jnp.sum(stream * stream, axis=1), "tp")
    scale_rms = lax.rsqrt(squares / D + eps)
    piece = lax.all_gather(scaled, "tp", axis=1, tiled=True)

    def project(weight):
        product = jnp.dot(piece, weight, preferred_element_type=jnp.float32)
        return (product * scale_rms[:, None]).astype(jnp.bfloat16)

    query = project(qkv_weight[0])
    keys = project(qkv_weight[1])
    values = project(qkv_weight[2])
    ends = jnp.cumsum(doc_lengths)
    first = lax.axis_index("ctx") * rows
    q_pos = first + jnp.arange(rows, dtype=jnp.int32)
    low = jnp.max(jnp.where(ends[None, :] <= q_pos[:, None], ends[None, :], 0), axis=1).astype(jnp.int32)
    attended = attention(query, keys, values, low, parts)
    return (mixed_stream, attended)


def solution(mesh):
    return jax.shard_map(
        body,
        mesh=mesh,
        in_specs=(
            P("ctx", "tp"),
            P(None, "ctx", "tp"),
            P("tp", None),
            P("tp"),
            P("tp"),
            P("tp", None),
            P(),
            P(None, None, "tp"),
            P(),
        ),
        out_specs=(P("ctx", "tp"), P("ctx", "tp")),
        check_vma=False,
    )
```

time: 292 us -> 262 us (0.90)
  waiting for transfers between devices: 124 us -> 71.4 us
  Pallas kernels: 69 us -> 114 us
  blocking collectives: 28.9 us -> 9.9 us
  local copies, waits for them, and re-layouts: 9.42 us -> 2.54 us
    all_gather x2 -> x0, waiting for transfers between devices: 50.6 us -> none  [the longest x1 44.1 us: body(): gated_all = lax.all_gather(gated, 'tp', axis=1, tiled=True)]
    pallas_call x2, Pallas kernels: 69 us -> 114 us  [the longest x1 60.7 us: attention(): pl.pallas_call(functools.partial(attention_kernel, devices), out_shape=ja...]
    all_to_all x1 -> x0, blocking collectives: 19.3 us -> none  [body(): moved = lax.all_to_all(mine, 'tp', split_axis=1, concat_axis=0, tiled=True)]
    conv_general_dilated x1, matrix products: 14.3 us -> 19.5 us  [body(): lax.conv_general_dilated(extended[None], kernel, (1,), [(0, 0)], dimensio...]
    transpose x1 -> x0, local copies, waits for them, and re-layouts: 4.95 us -> none  [body(): columns.reshape(parts, planes, share, local_width).transpose(1, 0, 2, 3)]
    ppermute x2, waiting for transfers between devices: 5.18 us -> 0.67 us  [shifted(): return lax.ppermute(value, axis, pairs)]
    dot_general x3, matrix products: 18 us -> 15 us  [project(): product = jnp.dot(piece, weight, preferred_element_type=jnp.float32)]
  transfers between devices with their start and end apart: 5 -> 3, of which waited for: 5 -> 2; matrix products, arithmetic and copies ran while one was open for 9% -> 2% of each run, Pallas kernels for 0% -> 0%
where the time goes in v2:
time: 262 us
  Pallas kernels  114 us (44%)
  waiting for transfers between devices  71.4 us (27%)
  matrix products  41.1 us (16%)
  between operations  14.2 us (5%)
  blocking collectives  9.9 us (4%)
  other arithmetic  4.71 us (2%)
  starting transfers between devices  3.88 us (1%)
    all_gather x1, waiting for transfers between devices, body(): piece = lax.all_gather(scaled, 'tp', axis=1, tiled=True)  70.7 us
    pallas_call x1, Pallas kernels, attention(): pl.pallas_call(functools.partial(attention_kernel, devices), out_shape=ja...  60.7 us
    pallas_call x1, Pallas kernels, deal(): pl.pallas_call(functools.partial(deal_kernel, devices, planes), out_shape...  53.1 us
    conv_general_dilated x1, matrix products, body(): lax.conv_general_dilated(extended[None], kernel, (1,), [(0, 0)], dimensio...  19.5 us
    dot_general x3, matrix products, project(): product = jnp.dot(piece, weight, preferred_element_type=jnp.float32)  15 us
    psum x1, blocking collectives, body(): squares = lax.psum(jnp.sum(stream * stream, axis=1), 'tp')  9.9 us
    dot_general x1, matrix products, body(): jnp.dot(gated_all, columns, preferred_element_type=jnp.float32)  6.67 us
  transfers between devices with their start and end apart: 3, of which 2 were waited for; matrix products, arithmetic and copies ran while one was open for 2% of the time, Pallas kernels for 0%

profile of v2, /device:TPU:6, one launch (start us, length us, event | category | flops | bytes accessed | tf_op | source)
XLA Modules:
  0.0 261.6 jit_solution(18362479213763978719)
XLA Ops:
  7.2 1.0 slice_bitcast_fusion.1
  8.2 1.9 collective-permute-start
  10.2 1.9 collective-permute-start.1
  12.1 1.3 multiply_bitcast_fusion
  13.5 0.7 neg.4
  14.2 1.1 exponential_multiply_fusion
  15.2 0.4 rev.3
  15.6 0.2 copy.17
  15.8 0.7 collective-permute-done.1
  16.5 0.1 maximum_bitcast_fusion
  16.7 19.5 %fusion.18 = f32[1,512,512]{2,0,1:T(1,128)S(1)} fusion(f32[128,1,512]{2,1,0:T(1,128)S(1)} %copy.17, f32[1,639,512]{2,1,0:T(8,128)S(1)} %maximum_bitcast_fusion), kind=kOutput, calls=%fused_computation.16 | convolution fusion | flops 402653184 | bytes 2619392 | tf_op jit(solution)/shard_map/conv_general_dilated | solution.py:377
  36.2 1.1 fusion.30.g_ref
  37.3 53.1 %deal_gated_and_columns.1 = (bf16[512,2048]{1,0:T(8,128)(2,1)}, bf16[2048,1024]{1,0:T(8,128)(2,1)}) custom-call(bf16[512,512]{1,0:T(8,128)(2,1)} %fusion.30.g_ref, bf16[512,4096]{1,0:T(8,128)(2,1)} %w_ref.1), custom_call_target="tpu_custom_call" | custom-call | tf_op jit(solution)/shard_map/deal_gated_and_columns/pallas_call | solution.py:181
  90.4 6.7 %multiply_reduce_fusion = (f32[512]{0:T(512)S(1)}, bf16[512,1024]{1,0:T(8,128)(2,1)}, bf16[512,1024]{1,0:T(8,128)(2,1)}) fusion(f32[1024]{0:T(1024)S(1)} %dynamic-slice-done, bf16[512,2048]{1,0:T(8,128)(2,1)} %get-tuple-element.4, bf16[2048,1024]{1,0:T(8,128)(2,1)} %get-tuple-element.5, bf16[512,1024]{1,0:T(8,128)(2,1)S(1)} %copy-done.3), kind=kOutput, calls=%fused_computation.9 | convolution fusion | flops 2151153152 | bytes 9443328 | tf_op jit(solution)/shard_map/dot_general | solution.py:393
  97.1 0.2 reduce-window.8
  97.3 0.1 select_reduce_fusion
  97.4 0.1 copy.18.low_ref
  97.6 9.9 %psum.7 = f32[512]{0:T(512)S(1)} all-reduce(f32[512]{0:T(512)S(1)} %get-tuple-element.6), channel_id=1, replica_groups=mesh['ctx'=8,'tp'=4] {'tp'}, use_global_device_ids=true, to_apply=%region_1.0 | all-reduce | flops 512 | bytes 4096 | tf_op jit(solution)/shard_map/psum | solution.py:396
  107.5 70.7 %all-gather.2.cloned.1.call-done = bf16[512,4096]{1,0:T(8,128)(2,1)} async-done(((bf16[512,1024]{1,0:T(8,128)(2,1)}), bf16[512,4096]{1,0:T(8,128)(2,1)}) %all-gather.2.cloned.1.call-update) | async-done | bytes 4194320 | tf_op jit(solution)/shard_map/all_gather | solution.py:398
  178.2 5.9 %fusion.20.v_ref = bf16[512,512]{1,0:T(8,128)(2,1)S(1)} fusion(bf16[512,4096]{1,0:T(8,128)(2,1)} %all-gather.2.cloned.1.call-done, bf16[3,4096,512]{2,1,0:T(8,128)(2,1)} %param.16, f32[512]{0:T(512)S(1)} %add_rsqrt_fusion), kind=kOutput, calls=%fused_computation.18 | convolution fusion | flops 2148007936 | bytes 8914944 | tf_op jit(solution)/shard_map/dot_general | solution.py:401
  184.1 4.5 %fusion.23.k_ref = bf16[512,512]{1,0:T(8,128)(2,1)S(1)} fusion(bf16[512,4096]{1,0:T(8,128)(2,1)S(1)} %copy-done.2, bf16[3,4096,512]{2,1,0:T(8,128)(2,1)} %param.16, f32[512]{0:T(512)S(1)} %add_rsqrt_fusion), kind=kOutput, calls=%fused_computation.19 | convolution fusion | flops 2148007936 | bytes 8914944 | tf_op jit(solution)/shard_map/dot_general | solution.py:401
  188.7 4.5 %fusion.26.q_ref = bf16[512,512]{1,0:T(8,128)(2,1)S(1)} fusion(bf16[512,4096]{1,0:T(8,128)(2,1)S(1)} %copy-done.2, bf16[3,4096,512]{2,1,0:T(8,128)(2,1)} %param.16, f32[512]{0:T(512)S(1)} %add_rsqrt_fusion), kind=kOutput, calls=%fused_computation.20 | convolution fusion | flops 2148007936 | bytes 8914944 | tf_op jit(solution)/shard_map/dot_general | solution.py:401
  193.2 60.7 %attention.1 = bf16[512,512]{1,0:T(8,128)(2,1)S(1)} custom-call(bf16[512,512]{1,0:T(8,128)(2,1)S(1)} %fusion.26.q_ref, bf16[512,512]{1,0:T(8,128)(2,1)S(1)} %fusion.23.k_ref, bf16[512,512]{1,0:T(8,128)(2,1)S(1)} %fusion.20.v_ref, s32[512,1]{1,0:T(8,128)S(1)} %copy.18.low_ref), custom_call_target="tpu_custom_call" | custom-call | tf_op jit(solution)/shard_map/attention/pallas_call | solution.py:325
  253.9 0.8 copy.24
  (18 shorter events, 0.1 us)
Async XLA Ops:
  7.2 171.0 %all-gather.2.cloned.1.call-start = ((), (), s32[]{:S(2)}) async-start(), calls=%async_computation | async-start | bytes 5242880 | tf_op jit(solution)/shard_map/all_gather | solution.py:398
  8.2 7.5 %collective-permute-start = (bf16[127,512]{1,0:T(8,128)(2,1)S(1)}, bf16[127,512]{1,0:T(8,128)(2,1)S(1)}, u32[]{:S(2)}, u32[]{:S(2)}) collective-permute-start(bf16[127,512]{1,0:T(8,128)(2,1)S(1)} %get-tuple-element.9), channel_id=1, source_target_pairs={{0,4},{4,8},{8,12},{12,16},{16,20},{20,24},{24,28},{1,5},{5,9},{9,... | collective-permute-start | bytes 390152 | tf_op jit(solution)/shard_map/ppermute | solution.py:347
  10.2 6.3 %collective-permute-start.1 = (bf16[127,512]{1,0:T(8,128)(2,1)S(1)}, bf16[127,512]{1,0:T(8,128)(2,1)S(1)}, u32[]{:S(2)}, u32[]{:S(2)}) collective-permute-start(bf16[127,512]{1,0:T(8,128)(2,1)S(1)} %get-tuple-element.10), channel_id=1, source_target_pairs={{0,4},{4,8},{8,12},{12,16},{16,20},{20,24},{24,28},{1,5},{5,9},{9,... | collective-permute-start | bytes 390152 | tf_op jit(solution)/shard_map/ppermute | solution.py:347
  16.6 19.5 %copy-start = (bf16[3,512,512]{2,1,0:T(8,128)(2,1)S(1)}, bf16[3,512,512]{2,1,0:T(8,128)(2,1)}, u32[]{:S(2)}) copy-start(bf16[3,512,512]{2,1,0:T(8,128)(2,1)} %param.10) | copy-start | bytes 4718596
  16.7 19.5 %copy-start.1 = (f32[512]{0:T(512)S(1)}, f32[512]{0:T(512)}, u32[]{:S(2)}) copy-start(f32[512]{0:T(512)} %param.13) | copy-start | bytes 6148
  36.2 54.2 %dynamic-slice-start = ((f32[4096]{0:T(1024)}, s32[]{:T(128)}), f32[1024]{0:T(1024)S(1)}, s32[]{:S(2)}) async-start(f32[4096]{0:T(1024)} %param.15, s32[]{:T(128)} %select_n.7), calls=%async_computation.1 | async-start | bytes 8704 | tf_op jit(solution)/shard_map/dynamic_slice | solution.py:390
  36.2 54.2 %copy-start.3 = (bf16[512,1024]{1,0:T(8,128)(2,1)S(1)}, bf16[512,1024]{1,0:T(8,128)(2,1)}, u32[]{:S(2)}) copy-start(bf16[512,1024]{1,0:T(8,128)(2,1)} %param.9) | copy-start | bytes 3145732
  90.4 6.7 %copy-start.4 = (s32[8]{0:T(128)S(1)}, s32[8]{0:T(128)}, u32[]{:S(2)}) copy-start(s32[8]{0:T(128)} %param.17) | copy-start | bytes 100
  178.2 5.9 %copy-start.2 = (bf16[512,4096]{1,0:T(8,128)(2,1)S(1)}, bf16[512,4096]{1,0:T(8,128)(2,1)}, u32[]{:S(2)}) copy-start(bf16[512,4096]{1,0:T(8,128)(2,1)} %all-gather.2.cloned.1.call-done) | copy-start | bytes 12582916
Sparse Core Ops, SparseCore 0:
  97.2 80.9 all-gather.1

commit v3 on v2

--- a/solution.py
+++ b/solution.py
@@ -207,9 +207,14 @@
     greet([{"ctx": p} for p in partners] + [{"ctx": mate}])
     outs = (k_all, v_all)
     ins = (k_ref, v_ref)
+    part = rows // 2
+    heads = cols // HS
 
     def slot(b, place):
-        return outs[b].at[pl.ds(pl.multiple_of(place * rows, rows), rows), :]
+        return outs[b % 2].at[pl.ds(pl.multiple_of(place * rows + (b // 2) * part, part), part), :]
+
+    def source(b):
+        return ins[b % 2].at[pl.ds((b // 2) * part, part), :]
 
     def to_partner(b, d, src, place, target):
         return send(src, slot(b, place), send_sem.at[b, d], recv_sem.at[b, d], {"ctx": target})
@@ -217,58 +222,56 @@
     def to_mate(b, d, src, place):
         return send(src, slot(b, place), mate_send.at[b, d], mate_recv.at[b, d], {"ctx": mate})
 
-    pair = min(2 * HS, cols)
-    pairs = cols // pair
-
-    def attend(place, at):
-        start = pl.multiple_of(place * rows, rows)
-        row = lax.broadcasted_iota(jnp.int32, (rows, rows), 0) + me * rows
-        column = lax.broadcasted_iota(jnp.int32, (rows, rows), 1) + start
-        allowed = (column <= row) & (column >= low_ref[...])
-        for inner in range(pair // HS):
-            lanes = pl.ds(pl.multiple_of(at * pair + inner * HS, HS), HS)
-            head = at * (pair // HS) + inner
+    def attend(place, side, causal):
+        start = pl.multiple_of(place * rows + side * part, part)
+        column = lax.broadcasted_iota(jnp.int32, (rows, part), 1) + start
+        allowed = column >= low_ref[...]
+        if causal:
+            row = lax.broadcasted_iota(jnp.int32, (rows, part), 0) + me * rows
+            allowed = allowed & (column <= row)
+        lanes = [pl.ds(h * HS, HS) for h in range(heads)]
+        tops = [top_ref[h] for h in range(heads)]
+        totals = [total_ref[h] for h in range(heads)]
+        sums = [accum_ref[:, lanes[h]] for h in range(heads)]
+        for h in range(heads):
             scores = lax.dot_general(
-                q_ref[:, lanes], k_all[pl.ds(start, rows), lanes], (((1,), (1,)), ((), ())),
+                q_ref[:, lanes[h]], k_all[pl.ds(start, part), lanes[h]], (((1,), (1,)), ((), ())),
                 preferred_element_type=jnp.float32)
             masked = jnp.where(allowed, scores * (HS ** (-0.5) * LOG2E), -1e30)
-            top = top_ref[head]
-            new_top = jnp.maximum(top, jnp.max(masked, axis=1, keepdims=True))
-            factor = jnp.exp2(top - new_top)
+            new_top = jnp.maximum(tops[h], jnp.max(masked, axis=1, keepdims=True))
+            factor = jnp.exp2(tops[h] - new_top)
             weights = jnp.exp2(masked - new_top)
-            total_ref[head] = total_ref[head] * factor + jnp.sum(weights, axis=1, keepdims=True)
-            accum_ref[:, lanes] = accum_ref[:, lanes] * factor + jnp.dot(
-                weights.astype(jnp.bfloat16), v_all[pl.ds(start, rows), lanes], preferred_element_type=jnp.float32)
-            top_ref[head] = new_top
-
-    def attend_chip(from_chip, first_core):
-        def step(i, unused):
-            place = from_chip * 2 + (first_core + i // pairs) % 2
-
-            @pl.when(place <= me)
-            def _():
-                attend(place, i % pairs)
-
-            return unused
-
-        lax.fori_loop(0, 2 * pairs, step, 0)
-
-    for b in range(2):
+            totals[h] = totals[h] * factor + jnp.sum(weights, axis=1, keepdims=True)
+            sums[h] = sums[h] * factor + jnp.dot(
+                weights.astype(jnp.bfloat16), v_all[pl.ds(start, part), lanes[h]],
+                preferred_element_type=jnp.float32)
+            tops[h] = new_top
+        for h in range(heads):
+            top_ref[h] = tops[h]
+            total_ref[h] = totals[h]
+            accum_ref[:, lanes[h]] = sums[h]
+
+    def attend_earlier(place, side):
+        @pl.when(place < me)
+        def _():
+            attend(place, side, False)
+
+    for b in range(4):
         for d in ((1, 2) if chips == 4 else tuple(range(1, chips))):
-            to_partner(b, d, ins[b], me, partners[d - 1]).start()
-        to_mate(b, 0, ins[b], me).start()
-        pltpu.make_async_copy(ins[b], slot(b, me), own_sem.at[b]).start()
+            to_partner(b, d, source(b), me, partners[d - 1]).start()
+        to_mate(b, 0, source(b), me).start()
+        pltpu.make_async_copy(source(b), slot(b, me), own_sem.at[b]).start()
     top_ref[...] = jnp.full(top_ref.shape, -1e20, jnp.float32)
     total_ref[...] = jnp.zeros(total_ref.shape, jnp.float32)
     accum_ref[...] = jnp.zeros(accum_ref.shape, jnp.float32)
 
-    def mate_landed(d):
-        for b in range(2):
+    def mate_landed(d, side):
+        for b in (2 * side, 2 * side + 1):
             place = flip(chip, d) * 2 + 1 - core
             to_mate(b, d, slot(b, place), place).wait_recv()
 
-    def partner_landed(d):
-        for b in range(2):
+    def partner_landed(d, side):
+        for b in (2 * side, 2 * side + 1):
             place = partners[d - 1]
             to_partner(b, d, slot(b, place), place, place).wait_recv()
             to_mate(b, d, slot(b, place), place).start()
@@ -278,44 +281,64 @@
                 def _():
                     to_partner(b, 3, slot(b, place), place, partners[2 - d]).start()
 
-    for b in range(2):
-        pltpu.make_async_copy(ins[b], slot(b, me), own_sem.at[b]).wait()
-    mate_landed(0)
-    attend_chip(chip, core)
+    for b in range(4):
+        pltpu.make_async_copy(source(b), slot(b, me), own_sem.at[b]).wait()
+
+    def own(side, unused):
+        attend(me, side, True)
+        return unused
+
+    lax.fori_loop(0, 2, own, 0)
+    for side in range(2):
+        mate_landed(0, side)
+
+    def beside(side, unused):
+        attend_earlier(mate, side)
+        return unused
+
+    lax.fori_loop(0, 2, beside, 0)
     if chips == 4:
-        for d in (1, 2):
-            partner_landed(d)
-        for d in (1, 2):
-            mate_landed(d)
-
-        def both(d, unused):
-            from_chip = (1 - d) * flip(chip, 1) + d * flip(chip, 2)
-            attend_chip(from_chip, 0)
-            return unused
-
-        lax.fori_loop(0, 2, both, 0)
-        partner_landed(3)
-        mate_landed(3)
-        attend_chip(flip(chip, 3), 0)
+        for side in range(2):
+            for d in (1, 2):
+                partner_landed(d, side)
+            for d in (1, 2):
+                mate_landed(d, side)
+
+            def near(i, unused):
+                from_chip = (1 - i // 2) * flip(chip, 1) + (i // 2) * flip(chip, 2)
+                attend_earlier(from_chip * 2 + i % 2, side)
+                return unused
+
+            lax.fori_loop(0, 4, near, 0)
+        for side in range(2):
+            partner_landed(3, side)
+            mate_landed(3, side)
+
+            def far(i, unused):
+                attend_earlier(flip(chip, 3) * 2 + i, side)
+                return unused
+
+            lax.fori_loop(0, 2, far, 0)
     else:
+        for side in range(2):
+            for d in range(1, chips):
+                partner_landed(d, side)
+            for d in range(1, chips):
+                mate_landed(d, side)
+
+            def later(i, unused):
+                attend_earlier(((chip + i // 2) % chips) * 2 + i % 2, side)
+                return unused
+
+            lax.fori_loop(2, 2 * chips, later, 0)
+    for h in range(heads):
+        lanes = pl.ds(h * HS, HS)
+        out_ref[:, lanes] = (accum_ref[:, lanes] / total_ref[h]).astype(out_ref.dtype)
+    for b in range(4):
         for d in range(1, chips):
-            partner_landed(d)
-        for d in range(1, chips):
-            mate_landed(d)
-
-        def later(d, unused):
-            attend_chip((chip + d) % chips, 0)
-            return unused
-
-        lax.fori_loop(1, chips, later, 0)
-    for head in range(cols // HS):
-        lanes = pl.ds(head * HS, HS)
-        out_ref[:, lanes] = (accum_ref[:, lanes] / total_ref[head]).astype(out_ref.dtype)
-    for b in range(2):
-        for d in range(1, chips):
-            to_partner(b, d, ins[b], me, partners[d - 1]).wait_send()
+            to_partner(b, d, source(b), me, partners[d - 1]).wait_send()
         for d in range(chips):
-            to_mate(b, d, ins[b], me).wait_send()
+            to_mate(b, d, source(b), me).wait_send()
 
 
 def attention(query, keys, values, low, devices):
@@ -333,12 +356,151 @@
             pltpu.VMEM((cols // HS, rows, 1), jnp.float32),
             pltpu.VMEM((cols // HS, rows, 1), jnp.float32),
             pltpu.VMEM((rows, cols), jnp.float32),
-            dma((2,)), dma((2, chips)), dma((2, chips)), dma((2, chips)), dma((2, chips)),
+            dma((4,)), dma((4, chips)), dma((4, chips)), dma((4, chips)), dma((4, chips)),
         ],
         compiler_params=pltpu.CompilerParams(
             collective_id=1, has_side_effects=True, vmem_limit_bytes=48 * 1024 * 1024),
         name="attention",
     )(query, keys, values, low[:, None])
+
+
+def project_kernel(planes, x_ref, sq_ref, w_ref, q_out, k_out, v_out, x_all, sq_all, w_all, total_ref,
+                   w_sem, x_send, x_recv, sq_send, sq_recv):
+    z = lax.axis_index("tp")
+    rows, width = x_ref.shape
+    half = width // 2
+    others = [(z + s) % planes for s in range(1, planes)]
+    greet([{"tp": t} for t in others])
+
+    def x_slot(origin, side):
+        return x_all.at[origin * 2 + side]
+
+    def hop(origin, side, sent, target):
+        place = x_slot(origin, side)
+        return send(place, place, x_send.at[sent, side], x_recv.at[origin, side], {"tp": target})
+
+    def first_hop(side, sent, target):
+        src = x_ref.at[:, pl.ds(side * half, half)]
+        return send(src, x_slot(z, side), x_send.at[sent, side], x_recv.at[z, side], {"tp": target})
+
+    def sq_copy(src, origin, target):
+        return send(src, sq_all.at[origin], sq_send.at[target], sq_recv.at[origin], {"tp": target})
+
+    def weights(origin):
+        rows_of = pl.ds(pl.multiple_of(origin * width, width), width)
+        return pltpu.make_async_copy(w_ref.at[:, rows_of, :], w_all.at[:, rows_of, :], w_sem.at[origin])
+
+    for t in others:
+        sq_copy(sq_ref, z, t).start()
+    for side in range(2):
+
+        @pl.when(z + 1 < planes)
+        def _():
+            first_hop(side, planes, z + 1).start()
+
+        @pl.when(z > 0)
+        def _():
+            first_hop(side, planes + 1, z - 1).start()
+
+    for s in range(planes):
+        weights((z + s) % planes).start()
+    total_ref[...] = jnp.zeros(total_ref.shape, jnp.float32)
+
+    def multiply(block, origin, side):
+        rows_of = pl.ds(pl.multiple_of(origin * width + side * half, half), half)
+
+        def one(j, unused):
+            total_ref[j] = total_ref[j] + jnp.dot(
+                block[...], w_all[j, rows_of, :], preferred_element_type=jnp.float32)
+            return unused
+
+        lax.fori_loop(0, 3, one, 0)
+
+    for s in range(planes):
+        weights((z + s) % planes).wait()
+    for side in range(2):
+        multiply(x_ref.at[:, pl.ds(side * half, half)], z, side)
+    for s in range(1, planes):
+        for side in range(2):
+
+            @pl.when(z - s >= 0)
+            def _():
+                hop(z - s, side, z - s, z).wait_recv()
+
+                @pl.when(z + 1 < planes)
+                def _():
+                    hop(z - s, side, z - s, z + 1).start()
+
+            @pl.when(z + s < planes)
+            def _():
+                hop(z + s, side, z + s, z).wait_recv()
+
+                @pl.when(z > 0)
+                def _():
+                    hop(z + s, side, z + s, z - 1).start()
+
+            @pl.when(z - s >= 0)
+            def _():
+                multiply(x_slot(z - s, side), z - s, side)
+
+            @pl.when(z + s < planes)
+            def _():
+                multiply(x_slot(z + s, side), z + s, side)
+
+    squares = sq_ref[0:1, :]
+    for t in others:
+        sq_copy(sq_all.at[t], t, t).wait_recv()
+        squares = squares + sq_all[t][0:1, :]
+    across = lax.broadcasted_iota(jnp.int32, (rows, rows), 0) == lax.broadcasted_iota(jnp.int32, (rows, rows), 1)
+    column = jnp.sum(jnp.where(across, jnp.broadcast_to(squares, (rows, rows)), 0.0), axis=1, keepdims=True)
+    scale = lax.rsqrt(column / D + eps)
+    for j, out in enumerate((q_out, k_out, v_out)):
+        out[...] = (total_ref[j] * scale).astype(out.dtype)
+    for t in others:
+        sq_copy(sq_ref, z, t).wait_send()
+    for side in range(2):
+
+        @pl.when(z + 1 < planes)
+        def _():
+            first_hop(side, planes, z + 1).wait_send()
+
+        @pl.when(z > 0)
+        def _():
+            first_hop(side, planes + 1, z - 1).wait_send()
+
+        for s in range(1, planes):
+
+            @pl.when((z - s >= 0) & (z + 1 < planes))
+            def _():
+                hop(z - s, side, z - s, z + 1).wait_send()
+
+            @pl.when((z + s < planes) & (z > 0))
+            def _():
+                hop(z + s, side, z + s, z - 1).wait_send()
+
+
+def project(scaled, squares, weight, planes):
+    rows, width = scaled.shape
+    cols = weight.shape[2]
+    dma = pltpu.SemaphoreType.DMA
+    vmem = pl.BlockSpec(memory_space=pltpu.VMEM)
+    result = jax.ShapeDtypeStruct((rows, cols), jnp.bfloat16)
+    return pl.pallas_call(
+        functools.partial(project_kernel, planes),
+        out_shape=(result,) * 3,
+        in_specs=[vmem, vmem, pl.BlockSpec(memory_space=pl.ANY)],
+        out_specs=[vmem] * 3,
+        scratch_shapes=[
+            pltpu.VMEM((planes * 2, rows, width // 2), jnp.bfloat16),
+            pltpu.VMEM((planes, 8, rows), jnp.float32),
+            pltpu.VMEM(weight.shape, weight.dtype),
+            pltpu.VMEM((3, rows, cols), jnp.float32),
+            dma((planes,)), dma((planes + 2, 2)), dma((planes, 2)), dma((planes,)), dma((planes,)),
+        ],
+        compiler_params=pltpu.CompilerParams(
+            collective_id=3, has_side_effects=True, vmem_limit_bytes=48 * 1024 * 1024),
+        name="project",
+    )(scaled, jnp.broadcast_to(squares[None, :], (8, rows)), weight)
 
 
 def shifted(value, axis, by):
@@ -393,17 +555,8 @@
     stream = residual_in.astype(jnp.float32) + jnp.dot(gated_all, columns, preferred_element_type=jnp.float32)
     mixed_stream = stream.astype(jnp.bfloat16)
     scaled = (stream * gain_local[None, :]).astype(jnp.bfloat16)
-    squares = lax.psum(jnp.sum(stream * stream, axis=1), "tp")
-    scale_rms = lax.rsqrt(squares / D + eps)
-    piece = lax.all_gather(scaled, "tp", axis=1, tiled=True)
-
-    def project(weight):
-        product = jnp.dot(piece, weight, preferred_element_type=jnp.float32)
-        return (product * scale_rms[:, None]).astype(jnp.bfloat16)
-
-    query = project(qkv_weight[0])
-    keys = project(qkv_weight[1])
-    values = project(qkv_weight[2])
+    squares = jnp.sum(stream * stream, axis=1)
+    query, keys, values = project(scaled, squares, qkv_weight, lax.axis_size("tp"))
     ends = jnp.cumsum(doc_lengths)
     first = lax.axis_index("ctx") * rows
     q_pos = first + jnp.arange(rows, dtype=jnp.int32)

time: 262 us -> 217 us (0.83)
  waiting for transfers between devices: 71.4 us -> 1.82 us
  Pallas kernels: 114 us -> 178 us
  matrix products: 41.1 us -> 25.8 us
  between operations: 14.2 us -> 0.86 us
  blocking collectives: 9.9 us -> 0 us
    pallas_call x0 -> x1, Pallas kernels: none -> 72.8 us  [project(): pl.pallas_call(functools.partial(project_kernel, planes), out_shape=(resu...]
    all_gather x1 -> x0, waiting for transfers between devices: 70.7 us -> none  [body(): piece = lax.all_gather(scaled, 'tp', axis=1, tiled=True)]
    dot_general x3 -> x0, matrix products: 15 us -> none  [project(): product = jnp.dot(piece, weight, preferred_element_type=jnp.float32)]
    psum x1 -> x0, blocking collectives: 9.9 us -> none  [body(): squares = lax.psum(jnp.sum(stream * stream, axis=1), 'tp')]
    pallas_call x1, Pallas kernels: 60.7 us -> 52.7 us  [attention(): pl.pallas_call(functools.partial(attention_kernel, devices), out_shape=ja...]
  transfers between devices with their start and end apart: 3 -> 2, of which waited for: 2 -> 1; matrix products, arithmetic and copies ran while one was open for 2% -> 1% of each run, Pallas kernels for 0% -> 0%
where the time goes in v3:
time: 217 us; the launch traced here: 216 us
  Pallas kernels  178 us (82%)
  matrix products  25.8 us (12%)
  starting transfers between devices  3.84 us (2%)
  other arithmetic  3.07 us (1%)
  local copies, waits for them, and re-layouts  2.58 us (1%)
    pallas_call x1, Pallas kernels, project(): pl.pallas_call(functools.partial(project_kernel, planes), out_shape=(resu...  72.8 us
    pallas_call x1, Pallas kernels, deal(): pl.pallas_call(functools.partial(deal_kernel, devices, planes), out_shape...  53 us
    pallas_call x1, Pallas kernels, attention(): pl.pallas_call(functools.partial(attention_kernel, devices), out_shape=ja...  52.7 us
    conv_general_dilated x1, matrix products, body(): lax.conv_general_dilated(extended[None], kernel, (1,), [(0, 0)], dimensio...  19.5 us
    dot_general x1, matrix products, body(): jnp.dot(gated_all, columns, preferred_element_type=jnp.float32)  6.29 us
  transfers between devices with their start and end apart: 2, of which 1 were waited for; matrix products, arithmetic and copies ran while one was open for 1% of the time, Pallas kernels for 0%

profile of v3, /device:TPU:6, one launch (start us, length us, event | category | flops | bytes accessed | tf_op | source)
XLA Modules:
  0.0 216.4 jit_solution(6098862163853300486)
XLA Ops:
  0.7 1.1 slice_bitcast_fusion.1
  1.7 1.9 collective-permute-start
  3.7 1.9 collective-permute-start.1
  5.6 1.3 multiply_bitcast_fusion
  7.0 0.1 exponential_multiply_fusion
  7.2 0.4 rev.3
  7.5 0.2 copy.17
  7.7 0.2 reduce-window.8
  7.9 0.1 select_reduce_fusion
  8.0 0.1 copy.18.low_ref
  8.1 0.0 collective-permute-done
  8.1 1.8 collective-permute-done.1
  10.0 0.1 maximum_bitcast_fusion
  10.1 0.0 copy-start
  10.1 0.0 copy-start.3
  10.2 19.5 %fusion = f32[1,512,512]{2,0,1:T(1,128)S(1)} fusion(f32[128,1,512]{2,1,0:T(1,128)S(1)} %copy.17, f32[1,639,512]{2,1,0:T(8,128)S(1)} %maximum_bitcast_fusion), kind=kOutput, calls=%fused_computation.4 | convolution fusion | flops 402653184 | bytes 2619392 | tf_op jit(solution)/shard_map/conv_general_dilated | solution.py:539
  29.7 1.1 fusion.3.g_ref
  30.8 53.0 %deal_gated_and_columns.1 = (bf16[512,2048]{1,0:T(8,128)(2,1)}, bf16[2048,1024]{1,0:T(8,128)(2,1)}) custom-call(bf16[512,512]{1,0:T(8,128)(2,1)} %fusion.3.g_ref, bf16[512,4096]{1,0:T(8,128)(2,1)} %w_ref.2), custom_call_target="tpu_custom_call" | custom-call | tf_op jit(solution)/shard_map/deal_gated_and_columns/pallas_call | solution.py:181
  83.8 0.0 dynamic-slice-done
  83.8 0.0 copy-done.4
  83.8 6.3 %multiply_reduce_fusion = (f32[512]{0:T(512)S(1)}, bf16[512,1024]{1,0:T(8,128)(2,1)S(1)}, bf16[512,1024]{1,0:T(8,128)(2,1)}) fusion(f32[1024]{0:T(1024)S(1)} %dynamic-slice-done, bf16[512,2048]{1,0:T(8,128)(2,1)} %get-tuple-element.7, bf16[2048,1024]{1,0:T(8,128)(2,1)} %get-tuple-element.8, bf16[512,1024]{1,0:T(8,128)(2,1)S(1)} %copy-done.4), kind=kOutput, calls=%fused_computation | convolution fusion | flops 2151153152 | bytes 9443328 | tf_op jit(solution)/shard_map/dot_general | solution.py:555
  90.1 72.8 %project.1 = (bf16[512,512]{1,0:T(8,128)(2,1)S(1)}, bf16[512,512]{1,0:T(8,128)(2,1)S(1)}, bf16[512,512]{1,0:T(8,128)(2,1)S(1)}) custom-call(bf16[512,1024]{1,0:T(8,128)(2,1)S(1)} %get-tuple-element.13.x_ref, f32[8,512]{1,0:T(8,128)S(1)} %broadcast_in_dim.16.sq_ref, bf16[3,4096,512]{2,1,0:T(8,128)(2,1)} %w_ref.3), custom_call_target="tpu_custom_call" | custom-call | tf_op jit(solution)/shard_map/project/pallas_call | solution.py:488
  162.9 52.7 %attention.1 = bf16[512,512]{1,0:T(8,128)(2,1)S(1)} custom-call(bf16[512,512]{1,0:T(8,128)(2,1)S(1)} %get-tuple-element.9.q_ref, bf16[512,512]{1,0:T(8,128)(2,1)S(1)} %get-tuple-element.10.k_ref, bf16[512,512]{1,0:T(8,128)(2,1)S(1)} %get-tuple-element.11.v_ref, s32[512,1]{1,0:T(8,128)S(1)} %copy.18.low_ref), custom_call_target="tpu_custom_call" | custom-call | tf_op jit(solution)/shard_map/attention/pallas_call | solution.py:348
  215.6 0.8 copy.24
  (14 shorter events, 0.1 us)
Async XLA Ops:
  0.6 6.3 %copy-start.2 = (f32[512]{0:T(512)S(1)}, f32[512]{0:T(512)}, u32[]{:S(2)}) copy-start(f32[512]{0:T(512)} %param.12) | copy-start | bytes 6148
  0.6 6.3 %copy-start.1 = (f32[512,128]{1,0:T(8,128)S(1)}, f32[512,128]{1,0:T(8,128)}, u32[]{:S(2)}) copy-start(f32[512,128]{1,0:T(8,128)} %param.11) | copy-start | bytes 786436
  0.7 7.0 %copy-start.5 = (s32[8]{0:T(128)S(1)}, s32[8]{0:T(128)}, u32[]{:S(2)}) copy-start(s32[8]{0:T(128)} %param.17) | copy-start | bytes 100
  1.7 6.4 %collective-permute-start = (bf16[127,512]{1,0:T(8,128)(2,1)S(1)}, bf16[127,512]{1,0:T(8,128)(2,1)S(1)}, u32[]{:S(2)}, u32[]{:S(2)}) collective-permute-start(bf16[127,512]{1,0:T(8,128)(2,1)S(1)} %get-tuple-element.15), channel_id=1, source_target_pairs={{0,4},{4,8},{8,12},{12,16},{16,20},{20,24},{24,28},{1,5},{5,9},{9,... | collective-permute-start | bytes 390152 | tf_op jit(solution)/shard_map/ppermute | solution.py:509
  3.7 6.3 %collective-permute-start.1 = (bf16[127,512]{1,0:T(8,128)(2,1)S(1)}, bf16[127,512]{1,0:T(8,128)(2,1)S(1)}, u32[]{:S(2)}, u32[]{:S(2)}) collective-permute-start(bf16[127,512]{1,0:T(8,128)(2,1)S(1)} %get-tuple-element.16), channel_id=1, source_target_pairs={{0,4},{4,8},{8,12},{12,16},{16,20},{20,24},{24,28},{1,5},{5,9},{9,... | collective-permute-start | bytes 390152 | tf_op jit(solution)/shard_map/ppermute | solution.py:509
  10.1 19.5 %copy-start = (bf16[3,512,512]{2,1,0:T(8,128)(2,1)S(1)}, bf16[3,512,512]{2,1,0:T(8,128)(2,1)}, u32[]{:S(2)}) copy-start(bf16[3,512,512]{2,1,0:T(8,128)(2,1)} %param.10) | copy-start | bytes 4718596
  10.1 19.5 %copy-start.3 = (f32[512]{0:T(512)S(1)}, f32[512]{0:T(512)}, u32[]{:S(2)}) copy-start(f32[512]{0:T(512)} %param.13) | copy-start | bytes 6148
  30.8 53.0 %dynamic-slice-start = ((f32[4096]{0:T(1024)}, s32[]{:T(128)}), f32[1024]{0:T(1024)S(1)}, s32[]{:S(2)}) async-start(f32[4096]{0:T(1024)} %param.15, s32[]{:T(128)} %select_n.7), calls=%async_computation | async-start | bytes 8704 | tf_op jit(solution)/shard_map/dynamic_slice | solution.py:552
  30.8 53.0 %copy-start.4 = (bf16[512,1024]{1,0:T(8,128)(2,1)S(1)}, bf16[512,1024]{1,0:T(8,128)(2,1)}, u32[]{:S(2)}) copy-start(bf16[512,1024]{1,0:T(8,128)(2,1)} %param.9) | copy-start | bytes 3145732

commit v4 on v3

--- a/solution.py
+++ b/solution.py
@@ -57,8 +57,10 @@
             pl.ds(pl.multiple_of(origin * depth + from_chip * rows, rows), rows),
             pl.ds(pl.multiple_of(from_core * half, half), half)]
 
-    def g_slot(origin):
-        return g_out.at[:, pl.ds(pl.multiple_of(origin * wide, wide), wide)]
+    part = wide // 2
+
+    def g_slot(origin, side):
+        return g_out.at[:, pl.ds(pl.multiple_of(origin * wide + side * part, part), part)]
 
     def to_plane(target):
         src = w_ref.at[
@@ -78,47 +80,51 @@
         place = slot(others[s], flip(chip, d), from_core)
         return send(place, place, m_send.at[s, d], m_recv.at[s, d], {"ctx": mate})
 
-    def hop(origin, sent, target):
-        place = g_slot(origin)
-        return send(place, place, g_send.at[sent], g_recv.at[origin], {"tp": target})
-
-    def first_hop(sent, target):
-        return send(g_ref, g_slot(z), g_send.at[sent], g_recv.at[z], {"tp": target})
+    def hop(origin, side, sent, target):
+        place = g_slot(origin, side)
+        return send(place, place, g_send.at[sent, side], g_recv.at[origin, side], {"tp": target})
+
+    def first_hop(side, sent, target):
+        src = g_ref.at[:, pl.ds(side * part, part)]
+        return send(src, g_slot(z, side), g_send.at[sent, side], g_recv.at[z, side], {"tp": target})
 
     for s in range(planes - 1):
         to_plane(others[s]).start()
 
-    @pl.when(z + 1 < planes)
-    def _():
-        first_hop(planes, z + 1).start()
-
-    @pl.when(z > 0)
-    def _():
-        first_hop(planes + 1, z - 1).start()
-
-    own = pltpu.make_async_copy(g_ref, g_slot(z), own_sem.at[0])
+    for side in range(2):
+
+        @pl.when(z + 1 < planes)
+        def _():
+            first_hop(side, planes, z + 1).start()
+
+        @pl.when(z > 0)
+        def _():
+            first_hop(side, planes + 1, z - 1).start()
+
+    own = pltpu.make_async_copy(
+        g_ref, g_out.at[:, pl.ds(pl.multiple_of(z * wide, wide), wide)], own_sem.at[0])
     own.start()
     kept = pltpu.make_async_copy(
         w_ref.at[:, pl.ds(pl.multiple_of(z * width, width), width)],
         w_out.at[pl.ds(pl.multiple_of(z * depth, depth), depth), :], own_sem.at[1])
     kept.start()
 
-    def relay(s):
+    def relay(s, side):
         @pl.when(z - s >= 0)
         def _():
-            hop(z - s, z - s, z).wait_recv()
+            hop(z - s, side, z - s, z).wait_recv()
 
             @pl.when(z + 1 < planes)
             def _():
-                hop(z - s, z - s, z + 1).start()
+                hop(z - s, side, z - s, z + 1).start()
 
         @pl.when(z + s < planes)
         def _():
-            hop(z + s, z + s, z).wait_recv()
+            hop(z + s, side, z + s, z).wait_recv()
 
             @pl.when(z > 0)
             def _():
-                hop(z + s, z + s, z - 1).start()
+                hop(z + s, side, z + s, z - 1).start()
 
     relayed = chips == 4
     direct = (1, 2) if relayed else tuple(range(1, chips))
@@ -127,7 +133,8 @@
         for d in direct:
             to_partner(s, d, chip, partners[d - 1]).start()
         to_mate(s, 0, core).start()
-    relay(1)
+    for side in range(2):
+        relay(1, side)
     for s in range(planes - 1):
         for d in direct:
             to_partner(s, d, flip(chip, d), partners[d - 1]).wait_recv()
@@ -138,7 +145,8 @@
                 def _():
                     to_partner(s, 3, flip(chip, d), partners[2 - d]).start()
     for s in range(2, planes):
-        relay(s)
+        for side in range(2):
+            relay(s, side)
     for s in range(planes - 1):
         if relayed:
             to_partner(s, 3, flip(chip, 3), partners[2]).wait_recv()
@@ -151,23 +159,26 @@
             to_mate(s, d, core).wait_send()
             to_mate(s, d, 1 - core).wait_recv()
 
-    @pl.when(z + 1 < planes)
-    def _():
-        first_hop(planes, z + 1).wait_send()
-
-    @pl.when(z > 0)
-    def _():
-        first_hop(planes + 1, z - 1).wait_send()
+    for side in range(2):
+
+        @pl.when(z + 1 < planes)
+        def _():
+            first_hop(side, planes, z + 1).wait_send()
+
+        @pl.when(z > 0)
+        def _():
+            first_hop(side, planes + 1, z - 1).wait_send()
 
     for s in range(1, planes):
-
-        @pl.when((z - s >= 0) & (z + 1 < planes))
-        def _():
-            hop(z - s, z - s, z + 1).wait_send()
-
-        @pl.when((z + s < planes) & (z > 0))
-        def _():
-            hop(z + s, z + s, z - 1).wait_send()
+        for side in range(2):
+
+            @pl.when((z - s >= 0) & (z + 1 < planes))
+            def _():
+                hop(z - s, side, z - s, z + 1).wait_send()
+
+            @pl.when((z + s < planes) & (z > 0))
+            def _():
+                hop(z + s, side, z + s, z - 1).wait_send()
 
     own.wait()
     kept.wait()
@@ -187,7 +198,7 @@
         in_specs=[pl.BlockSpec(memory_space=pl.ANY)] * 2,
         out_specs=[pl.BlockSpec(memory_space=pl.ANY)] * 2,
         scratch_shapes=[
-            dma((2,)), dma((planes + 2,)), dma((planes,)), dma((planes,)), dma((planes,)),
+            dma((2,)), dma((planes + 2, 2)), dma((planes, 2)), dma((planes,)), dma((planes,)),
             dma((planes - 1, chips)), dma((planes - 1, chips)), dma((planes - 1, chips)), dma((planes - 1, chips)),
         ],
         compiler_params=pltpu.CompilerParams(collective_id=2, has_side_effects=True),
@@ -527,9 +538,7 @@
     query_h = features[0]
     key_h = features[1]
     value_h = features[2]
-    edge_keys, edge_values = shifted(
-        (key_h[rows - (span - 1) :], value_h[rows - (span - 1) :]), "ctx", 1
-    )
+    edge_keys, edge_values = shifted(features[1:, rows - (span - 1) :], "ctx", 1)
     mixed_in = key_h.astype(jnp.float32) * value_h.astype(jnp.float32)
     before = edge_keys.astype(jnp.float32) * edge_values.astype(jnp.float32)
     extended = jnp.concatenate([before, mixed_in], axis=0)

time: 217 us -> 214 us (0.986)
  transfers between devices with their start and end apart: 2 -> 1, of which waited for: 1 -> 1; matrix products, arithmetic and copies ran while one was open for 1% -> 1% of each run, Pallas kernels for 0% -> 0%
where the time goes in v4:
time: 214 us
  Pallas kernels  177 us (83%)
  matrix products  25.8 us (12%)
  other arithmetic  3.49 us (2%)
  waiting for transfers between devices  2.83 us (1%)
  local copies, waits for them, and re-layouts  2.63 us (1%)
    pallas_call x1, Pallas kernels, project(): pl.pallas_call(functools.partial(project_kernel, planes), out_shape=(resu...  72.1 us
    pallas_call x1, Pallas kernels, deal(): pl.pallas_call(functools.partial(deal_kernel, devices, planes), out_shape...  53 us
    pallas_call x1, Pallas kernels, attention(): pl.pallas_call(functools.partial(attention_kernel, devices), out_shape=ja...  51.6 us
    conv_general_dilated x1, matrix products, body(): lax.conv_general_dilated(extended[None], kernel, (1,), [(0, 0)], dimensio...  19.5 us
    dot_general x1, matrix products, body(): jnp.dot(gated_all, columns, preferred_element_type=jnp.float32)  6.29 us
  transfers between devices with their start and end apart: 1, of which 1 were waited for; matrix products, arithmetic and copies ran while one was open for 1% of the time, Pallas kernels for 0%

profile of v4, /device:TPU:6, one launch (start us, length us, event | category | flops | bytes accessed | tf_op | source)
XLA Modules:
  0.0 214.2 jit_solution(7346408494281850056)
XLA Ops:
  0.6 0.0 copy-start
  0.6 1.1 slice.13
  1.8 1.9 collective-permute-start
  3.7 0.7 neg.4
  4.4 1.1 exponential_multiply_fusion
  5.5 0.4 rev.3
  5.9 0.2 copy.17
  6.1 0.0 copy-done.3
  6.1 0.2 reduce-window.8
  6.2 0.1 select_reduce_fusion
  6.3 0.1 copy.18.low_ref
  6.5 0.1 multiply_bitcast_fusion
  6.7 2.8 %collective-permute-done = bf16[2,127,512]{2,1,0:T(8,128)(2,1)S(1)} collective-permute-done((bf16[2,127,512]{2,1,0:T(8,128)(2,1)S(1)}, bf16[2,127,512]{2,1,0:T(8,128)(2,1)S(1)}, u32[]{:S(2)}, u32[]{:S(2)}) %collective-permute-start) | collective-permute-done | bytes 260128 | tf_op jit(solution)/shard_map/ppermute | solution.py:520
  9.5 0.1 maximum_bitcast_fusion
  9.7 0.0 copy-start.1
  9.7 19.5 %fusion = f32[1,512,512]{2,0,1:T(1,128)S(1)} fusion(f32[128,1,512]{2,1,0:T(1,128)S(1)} %copy.17, f32[1,639,512]{2,1,0:T(8,128)S(1)} %maximum_bitcast_fusion), kind=kOutput, calls=%fused_computation.4 | convolution fusion | flops 402653184 | bytes 2619392 | tf_op jit(solution)/shard_map/conv_general_dilated | solution.py:548
  29.2 1.1 fusion.3.g_ref
  30.3 53.0 %deal_gated_and_columns.1 = (bf16[512,2048]{1,0:T(8,128)(2,1)}, bf16[2048,1024]{1,0:T(8,128)(2,1)}) custom-call(bf16[512,512]{1,0:T(8,128)(2,1)} %fusion.3.g_ref, bf16[512,4096]{1,0:T(8,128)(2,1)} %w_ref.2), custom_call_target="tpu_custom_call" | custom-call | tf_op jit(solution)/shard_map/deal_gated_and_columns/pallas_call | solution.py:192
  83.4 0.0 dynamic-slice-done
  83.4 0.0 copy-done.2
  83.4 6.3 %multiply_reduce_fusion = (f32[512]{0:T(512)S(1)}, bf16[512,1024]{1,0:T(8,128)(2,1)S(1)}, bf16[512,1024]{1,0:T(8,128)(2,1)}) fusion(f32[1024]{0:T(1024)S(1)} %dynamic-slice-done, bf16[512,2048]{1,0:T(8,128)(2,1)} %get-tuple-element.7, bf16[2048,1024]{1,0:T(8,128)(2,1)} %get-tuple-element.8, bf16[512,1024]{1,0:T(8,128)(2,1)S(1)} %copy-done.2), kind=kOutput, calls=%fused_computation | convolution fusion | flops 2151153152 | bytes 9443328 | tf_op jit(solution)/shard_map/dot_general | solution.py:564
  89.7 72.1 %project.1 = (bf16[512,512]{1,0:T(8,128)(2,1)S(1)}, bf16[512,512]{1,0:T(8,128)(2,1)S(1)}, bf16[512,512]{1,0:T(8,128)(2,1)S(1)}) custom-call(bf16[512,1024]{1,0:T(8,128)(2,1)S(1)} %get-tuple-element.13.x_ref, f32[8,512]{1,0:T(8,128)S(1)} %broadcast_in_dim.16.sq_ref, bf16[3,4096,512]{2,1,0:T(8,128)(2,1)} %w_ref.3), custom_call_target="tpu_custom_call" | custom-call | tf_op jit(solution)/shard_map/project/pallas_call | solution.py:499
  161.7 51.6 %attention.1 = bf16[512,512]{1,0:T(8,128)(2,1)S(1)} custom-call(bf16[512,512]{1,0:T(8,128)(2,1)S(1)} %get-tuple-element.9.q_ref, bf16[512,512]{1,0:T(8,128)(2,1)S(1)} %get-tuple-element.10.k_ref, bf16[512,512]{1,0:T(8,128)(2,1)S(1)} %get-tuple-element.11.v_ref, s32[512,1]{1,0:T(8,128)S(1)} %copy.18.low_ref), custom_call_target="tpu_custom_call" | custom-call | tf_op jit(solution)/shard_map/attention/pallas_call | solution.py:359
  213.4 0.8 copy.24
  (8 shorter events, 0.0 us)
Async XLA Ops:
  0.6 5.9 %copy-start = (bf16[3,512,512]{2,1,0:T(8,128)(2,1)S(1)}, bf16[3,512,512]{2,1,0:T(8,128)(2,1)}, u32[]{:S(2)}) copy-start(bf16[3,512,512]{2,1,0:T(8,128)(2,1)} %param.10) | copy-start | bytes 4718596
  0.6 5.4 %copy-start.3 = (s32[8]{0:T(128)S(1)}, s32[8]{0:T(128)}, u32[]{:S(2)}) copy-start(s32[8]{0:T(128)} %param.17) | copy-start | bytes 100
  1.8 7.7 %collective-permute-start = (bf16[2,127,512]{2,1,0:T(8,128)(2,1)S(1)}, bf16[2,127,512]{2,1,0:T(8,128)(2,1)S(1)}, u32[]{:S(2)}, u32[]{:S(2)}) collective-permute-start(bf16[2,127,512]{2,1,0:T(8,128)(2,1)S(1)} %slice.13), channel_id=1, source_target_pairs={{0,4},{4,8},{8,12},{12,16},{16,20},{20,24},{24,28},{1,5},{5,9},{9,... | collective-permute-start | bytes 780296 | tf_op jit(solution)/shard_map/ppermute | solution.py:520
  9.7 19.5 %copy-start.1 = (f32[512]{0:T(512)S(1)}, f32[512]{0:T(512)}, u32[]{:S(2)}) copy-start(f32[512]{0:T(512)} %param.13) | copy-start | bytes 6148
  30.3 53.1 %dynamic-slice-start = ((f32[4096]{0:T(1024)}, s32[]{:T(128)}), f32[1024]{0:T(1024)S(1)}, s32[]{:S(2)}) async-start(f32[4096]{0:T(1024)} %param.15, s32[]{:T(128)} %select_n.7), calls=%async_computation | async-start | bytes 8704 | tf_op jit(solution)/shard_map/dynamic_slice | solution.py:561
  30.3 53.1 %copy-start.2 = (bf16[512,1024]{1,0:T(8,128)(2,1)S(1)}, bf16[512,1024]{1,0:T(8,128)(2,1)}, u32[]{:S(2)}) copy-start(bf16[512,1024]{1,0:T(8,128)(2,1)} %param.9) | copy-start | bytes 3145732
